TPU v7x, 512 devices: a whole 4x8x8 slice. The times are simulated.
512 devices in a mesh: shot: 32 (over y, x), px: 4 (over z_lo, core), py: 4 (over z_hi).
Axes of the slice: x: 4, y: 8, z: 8 (z_hi: 4, z_lo: 2; z = z_hi * 2 + z_lo), core: 2. Of those that a mesh axis runs over, the one named last changes fastest.
Arguments:
- fwd_now: float32 [32, 128, 64, 256], P('shot', 'px', 'py'), may hold values from -6 to 6
- fwd_next: float32 [32, 128, 64, 256], P('shot', 'px', 'py'), may hold values from -6 to 6
- adj_now: float32 [32, 128, 64, 256], P('shot', 'px', 'py'), may hold values from -6 to 6
- adj_next: float32 [32, 128, 64, 256], P('shot', 'px', 'py'), may hold values from -6 to 6
- velocity: float32 [128, 128, 1024], P('shot', 'px', 'py'), may hold values from 1.5 to 4.5
- density: float32 [128, 128, 1024], P('shot', 'px', 'py'), may hold values from 1 to 2.6
- gradient_in: float32 [128, 128, 1024], P('shot', 'px', 'py'), may hold values from -6 to 6
- block_home: int32 [8, 16], replicated, may hold values from 0 to 127, as said below
- aperture_col: int32 [32], P('shot'), may hold values from 0 to 7
- source_cell: int32 [32], P('shot'), may hold values from 0 to 2097151
- source_amp: float32 [32], P('shot'), may hold values from -6 to 6
- receiver_cell: int32 [32, 256], P('shot'), may hold values from 0 to 2097151
- receiver_residual: float32 [32, 256], P('shot'), may hold values from -6 to 6
Outputs:
- fwd_prev: float32 [32, 128, 64, 256], P('shot', 'px', 'py')
- adj_prev: float32 [32, 128, 64, 256], P('shot', 'px', 'py')
- gradient: float32 [128, 128, 1024], P('shot', 'px', 'py')
Inputs may be any that keep to these rules, and one draw needn't show every extreme that they name: `block_home`: each of the 8 columns has its 16 depth blocks on 16 different owners, the owner of block b being b // 4; every model block index appears exactly once.
All inputs are finite; a program needn't handle non-finite values.
Results may differ from a plain program's by a relative error of at most 0.000092.
Values sent between devices are 32-bit elements; how exact they have to be, the bound alone decides.
A program may use at most 64 MiB of HBM per device.

v0:
```python
import jax
import jax.numpy as jnp
from jax import lax
from jax.sharding import PartitionSpec as P

COEFS = (1225.0 / 1024.0, -245.0 / 3072.0, 49.0 / 5120.0, -5.0 / 7168.0)
COURANT2 = 0.01


def with_halo(array, sides, width):
    for axis, dim in sides:
        devices, length = (lax.axis_size(axis), array.shape[dim])
        up = [(i, (i + 1) % devices) for i in range(devices - 1)]
        down = [(j, i) for i, j in up]
        last = lax.slice_in_dim(array, length - width, length, axis=dim)
        first = lax.slice_in_dim(array, 0, width, axis=dim)
        before = lax.ppermute(last, axis, up)
        after = lax.ppermute(first, axis, down)
        array = jnp.concatenate([before, array, after], axis=dim)
    return array


def from_behind(array, axis, by):
    devices = lax.axis_size(axis)
    pairs = [(i, i + by) for i in range(devices) if 0 <= i + by < devices]
    return lax.ppermute(array, axis, pairs)


def cut(values, begin, length, along):
    return lax.slice_in_dim(values, begin, begin + length, axis=along)


def forward_diff(extended, offset, first_face, face_count, along):
    summed = None
    for reach, weight in enumerate(COEFS, 1):
        term = weight * (
            cut(extended, first_face + reach + offset, face_count, along)
            - cut(extended, first_face + 1 - reach + offset, face_count, along)
        )
        summed = term if summed is None else summed + term
    return summed


def backward_diff(extended, offset, cell_count, along):
    summed = None
    for reach, weight in enumerate(COEFS, 1):
        term = weight * (
            cut(extended, reach - 1 + offset, cell_count, along)
            - cut(extended, offset - reach, cell_count, along)
        )
        summed = term if summed is None else summed + term
    return summed


def face_flux(forward, rho_low, rho_high, face_index, total_cells, along_three):
    mask_shape = [1, 1, 1]
    mask_shape[along_three] = face_index.shape[0]
    inside = ((face_index >= 0) & (face_index <= total_cells - 2)).reshape(mask_shape)
    safe = jnp.where(inside, rho_low + rho_high, 1.0)
    return jnp.where(inside, 2.0 * forward / safe, 0.0)


def depth_term(fields, density):
    cells = fields.shape[3]
    forward = forward_diff(jnp.pad(fields, ((0, 0), (0, 0), (0, 0), (3, 4))), 3, 0, cells, 3)
    rho_ext = jnp.pad(density, ((0, 0), (0, 0), (0, 1)))
    flux = face_flux(
        forward,
        cut(rho_ext, 0, cells, 2),
        cut(rho_ext, 1, cells, 2),
        jnp.arange(cells, dtype=jnp.int32),
        cells,
        2,
    )
    return backward_diff(jnp.pad(flux, ((0, 0), (0, 0), (0, 0), (4, 3))), 4, cells, 3)


def place(field, cells, values, pos_x, pos_y, span_y):
    rows_x, rows_y, depth = field.shape
    col_x = cells // (span_y * depth)
    col_y = cells // depth % span_y
    col_z = cells % depth
    loc_x = col_x - pos_x * rows_x
    loc_y = col_y - pos_y * rows_y
    inside = (loc_x >= 0) & (loc_x < rows_x) & (loc_y >= 0) & (loc_y < rows_y)
    return field.at[jnp.clip(loc_x, 0, rows_x - 1), jnp.clip(loc_y, 0, rows_y - 1), col_z].add(
        jnp.where(inside, values, 0.0)
    )


def shards(
    fwd_now,
    fwd_next,
    adj_now,
    adj_next,
    velocity,
    density,
    gradient_in,
    block_home,
    aperture_col,
    source_cell,
    source_amp,
    receiver_cell,
    receiver_residual,
):
    rows_x, rows_y, depth = fwd_now.shape[1:]
    owners_count = lax.axis_size("shot")
    held = velocity.shape[0]
    blocks = block_home.shape[1]
    slab_depth = depth // blocks
    pos_x = lax.axis_index("px")
    pos_y = lax.axis_index("py")
    span_x = rows_x * lax.axis_size("px")
    span_y = rows_y * lax.axis_size("py")
    wanted = block_home[aperture_col[0]]
    owner_of = wanted // held
    peers = jnp.arange(owners_count, dtype=jnp.int32)
    hits = owner_of[None, :] == peers[:, None]
    request = jnp.sum(jnp.where(hits, wanted[None, :] % held + 1, 0), axis=1) - 1
    asked = lax.all_to_all(request[:, None], "shot", split_axis=0, concat_axis=0, tiled=True)[:, 0]
    served = (asked >= 0)[:, None, None]
    row_pick = jnp.clip(asked, 0, held - 1)
    outgoing = (
        jnp.where(served, velocity[row_pick], 0.0),
        jnp.where(served, density[row_pick], 0.0),
    )
    got_vel, got_dens = (
        lax.all_to_all(outgoing[0], "shot", split_axis=0, concat_axis=0, tiled=True),
        lax.all_to_all(outgoing[1], "shot", split_axis=0, concat_axis=0, tiled=True),
    )
    vel_slabs = got_vel[owner_of]
    dens_slabs = got_dens[owner_of]

    def to_pencil(slabs):
        return (
            slabs.reshape(blocks, rows_x, rows_y, slab_depth)
            .transpose(1, 2, 0, 3)
            .reshape(rows_x, rows_y, depth)
        )

    vel = to_pencil(vel_slabs)
    dens = to_pencil(dens_slabs)
    fields = jnp.stack([fwd_now[0], adj_now[0]])
    face_x = pos_x * rows_x + jnp.arange(rows_x, dtype=jnp.int32)
    face_y = pos_y * rows_y + jnp.arange(rows_y, dtype=jnp.int32)
    padded = with_halo(fields, (("px", 1), ("py", 2)), 4)
    next_x = from_behind(dens[0], "px", -1)
    next_y = from_behind(dens[:, 0], "py", -1)
    rho_x = jnp.concatenate([dens, next_x[None]], axis=0)
    rho_y = jnp.concatenate([dens, next_y[:, None]], axis=1)
    forward_x = forward_diff(padded[:, :, 4 : 4 + rows_y], 4, 0, rows_x, 1)
    flux_x = face_flux(forward_x, rho_x[:rows_x], rho_x[1:], face_x, span_x, 0)
    wide_x = with_halo(flux_x, (("px", 1),), 4)
    div_x = backward_diff(wide_x, 4, rows_x, 1)
    forward_y = forward_diff(padded[:, 4 : 4 + rows_x], 4, 0, rows_y, 2)
    flux_y = face_flux(forward_y, rho_y[:, :rows_y], rho_y[:, 1:], face_y, span_y, 1)
    wide_y = with_halo(flux_y, (("py", 2),), 4)
    div_y = backward_diff(wide_y, 4, rows_y, 2)
    lap = div_x + div_y + depth_term(fields, dens)
    update = COURANT2 * (dens * vel * vel) * lap
    fwd_new = 2.0 * fwd_now[0] - fwd_next[0] + update[0]
    adj_new = 2.0 * adj_now[0] - adj_next[0] + update[1]
    fwd_new = place(fwd_new, source_cell, -source_amp, pos_x, pos_y, span_y)
    adj_new = place(adj_new, receiver_cell[0], receiver_residual[0], pos_x, pos_y, span_y)
    contribution = 2.0 / vel * adj_now[0] * (fwd_next[0] - 2.0 * fwd_now[0] + fwd_new)
    slabs_out = (
        contribution.reshape(rows_x, rows_y, blocks, slab_depth)
        .transpose(2, 0, 1, 3)
        .reshape(blocks, rows_x, rows_y * slab_depth)
    )
    sending = (
        jnp.zeros((owners_count,) + slabs_out.shape[1:], jnp.float32).at[owner_of].set(slabs_out)
    )
    arrived = lax.all_to_all(sending, "shot", split_axis=0, concat_axis=0, tiled=True)
    chooser = (asked[None, :] == jnp.arange(held, dtype=jnp.int32)[:, None]).astype(jnp.float32)
    gradient = gradient_in + jnp.einsum(
        "sr,rxy->sxy", chooser, arrived, precision=lax.Precision.HIGHEST
    )
    return (fwd_new[None], adj_new[None], gradient)


def solution(mesh):
    in_specs = (
        P("shot", "px", "py", None),
        P("shot", "px", "py", None),
        P("shot", "px", "py", None),
        P("shot", "px", "py", None),
        P("shot", "px", "py"),
        P("shot", "px", "py"),
        P("shot", "px", "py"),
        P(),
        P("shot"),
        P("shot"),
        P("shot"),
        P("shot", None),
        P("shot", None),
    )
    out_specs = (P("shot", "px", "py", None), P("shot", "px", "py", None), P("shot", "px", "py"))
    return jax.shard_map(shards, mesh=mesh, in_specs=in_specs, out_specs=out_specs, check_vma=False)
```

profile of v0, /device:TPU:130, one launch (start us, length us, event | category | flops | bytes accessed | tf_op | source)
XLA Modules:
  0.0 227.8 jit_solution(12392704099558187609)
XLA Ops:
  2.2 18.6 %all_to_all.21 = s32[32,1,1]{2,1,0:T(1,128)S(1)} all-to-all(s32[32,1,1]{2,1,0:T(1,128)S(1)} %copy.99), channel_id=1, replica_groups=mesh['shot'=32,'px'=4,'py'=4] {'shot'}, dimensions={0} | all-to-all | bytes 256 | tf_op jit(solution)/shard_map/all_to_all | solution.py:120
  25.5 31.2 %all_to_all.22 = f32[32,32,256]{2,1,0:T(8,128)S(1)} all-to-all(f32[32,32,256]{2,1,0:T(8,128)S(1)} %get-tuple-element.55), channel_id=1, replica_groups=mesh['shot'=32,'px'=4,'py'=4] {'shot'}, dimensions={0} | all-to-all | bytes 2097152 | tf_op jit(solution)/shard_map/all_to_all | solution.py:129
  56.8 5.8 %all-to-all-start.2 = ((f32[32,32,256]{2,1,0:T(8,128)}), f32[32,32,256]{2,1,0:T(8,128)}, u32[]{:S(2)}, u32[]{:S(2)}) async-start(f32[32,32,256]{2,1,0:T(8,128)} %get-tuple-element.54), calls=%async_computation.2 | async-start | bytes 2097152 | tf_op jit(solution)/shard_map/all_to_all | solution.py:128
  72.7 6.8 %collective-permute-start.6 = (f32[2,40,4,256]{3,2,1,0:T(4,128)}, f32[2,40,4,256]{3,2,1,0:T(4,128)}, u32[]{:S(2)}, u32[]{:S(2)}) collective-permute-start(f32[2,40,4,256]{3,2,1,0:T(4,128)} %get-tuple-element.43), channel_id=1, source_target_pairs={{0,1},{1,2},{2,3},{4,5},{5,6},{6,7},{8,9},{9,10},{10,11},{12,13},{... | collective-permute-start | bytes 983048 | tf_op jit(solution)/shard_map/ppermute | solution.py:17
  84.4 3.8 %copy.105 = f32[1,16,16,16]{3,2,1,0:T(8,128)} copy(f32[1,16,16,16]{0,3,1,2:T(8,128)} %bitcast.103) | data formatting | bytes 32768 | tf_op jit(solution)/shard_map/slice | solution.py:147
  93.7 3.4 %pad_maximum_fusion.2 = (f32[2,40,20,256]{3,2,1,0:T(8,128)}, f32[2,40,20,256]{3,2,1,0:T(8,128)}) fusion(f32[2,40,4,256]{3,2,1,0:T(4,128)} %collective-permute-done.5, f32[2,4,16,256]{3,2,1,0:T(8,128)S(1)} %collective-permute-done, f32[2,32,16,256]{3,2,1,0:T(8,128)S(1)} %constant_dynamic-update-slice_fusion, f32[2,4,16,256]{3,2,1,0:T(8,128)S(1)} %collective-permute-done.1, ...), kind=kLoop, calls=%fused_computation.42 | loop fusion | flops 2457600 | bytes 5242880 | tf_op jit(solution)/shard_map/concatenate | solution.py:19
  97.2 2.7 %gather_fusion.3 = f32[16,32,256]{2,1,0:T(8,128)} fusion(f32[32,32,256]{2,1,0:T(8,128)} %all-to-all-done.2, s32[1024]{0:T(1024)} %copy-done.14), kind=kCustom, calls=%fused_computation.3 | custom fusion | bytes 1048640 | tf_op jit(solution)/shard_map/gather | solution.py:131
  99.9 3.0 %copy.102 = f32[16,32,256]{1,2,0:T(8,128)} copy(f32[16,32,256]{2,1,0:T(8,128)} %gather_fusion.3) | data formatting | bytes 1048576 | tf_op jit(solution)/shard_map/gather | solution.py:131
  102.8 3.2 %copy.103 = f32[32,16,16,16]{0,3,2,1:T(8,128)} copy(f32[32,16,16,16]{0,3,1,2:T(8,128)} %bitcast.105) | data formatting | bytes 1048576 | tf_op jit(solution)/shard_map/transpose | solution.py:137
  108.1 5.8 %fusion.1 = (f32[32,16,256]{0,2,1:T(8,128)}, f32[32,16,256]{0,2,1:T(8,128)}, f32[32,16,256]{0,2,1:T(8,128)}) fusion(f32[32,16,256]{0,2,1:T(8,128)S(1)} %bitcast.100, pred[256]{0:T(512)(128)(4,1)} %iota_compare_fusion.2, f32[1,16,256]{0,2,1:T(8,128)} %copy.106, pred[32]{0:T(512)(128)(4,1)} %compare_and_fusion.1, f32[32,1,256]{0,2,1:T(8,128)} %bitcast.16, ...), kind=kLoop, calls=%fused_computation.28 | loop fusion | flops 1048576 | bytes 2146608 | tf_op jit(solution)/shard_map/jit(_where)/select_n | solution.py:59
  113.9 3.0 %copy.107 = f32[32,16,256]{2,1,0:T(8,128)} copy(f32[32,16,256]{0,2,1:T(8,128)} %get-tuple-element.38) | data formatting | bytes 1048576 | tf_op jit(solution)/shard_map/jit(_where)/select_n | solution.py:59
  116.9 2.9 %fusion.96 = f32[2,32,16,256]{3,2,1,0:T(8,128)S(1)} fusion(f32[2,32,16,256]{3,2,1,0:T(8,128)S(1)} %constant_dynamic-update-slice_fusion, f32[2,4,16,256]{3,2,1,0:T(8,128)S(1)} %collective-permute-done.1, f32[2,4,16,256]{3,2,1,0:T(8,128)S(1)} %collective-permute-done, f32[32,16,256]{2,1,0:T(8,128)} %copy.107, pred[32]{0:T(512)(128)(4,1)S(1)} %copy-done.17), kind=kLoop, calls=%fused_computation.163 | loop fusion | flops 5505024 | bytes 2883616 | tf_op jit(solution)/shard_map/jit(_where)/select_n | solution.py:60
  122.8 3.0 %copy.109 = f32[32,16,256]{2,1,0:T(8,128)} copy(f32[32,16,256]{0,2,1:T(8,128)} %get-tuple-element.37) | data formatting | bytes 1048576 | tf_op jit(solution)/shard_map/jit(_where)/select_n | solution.py:59
  125.8 3.0 %copy.108 = f32[32,16,256]{2,1,0:T(8,128)} copy(f32[32,16,256]{0,2,1:T(8,128)} %get-tuple-element.39) | data formatting | bytes 1048576 | tf_op jit(solution)/shard_map/jit(_where)/select_n | solution.py:59
  128.9 7.1 %collective-permute-start.3 = (f32[2,4,16,256]{3,2,1,0:T(8,128)}, f32[2,4,16,256]{3,2,1,0:T(8,128)}, u32[]{:S(2)}, u32[]{:S(2)}) collective-permute-start(f32[2,4,16,256]{3,2,1,0:T(8,128)} %get-tuple-element.48), channel_id=1, source_target_pairs={{0,4},{4,8},{8,12},{1,5},{5,9},{9,13},{2,6},{6,10},{10,14},{3,7},{... | collective-permute-start | bytes 393224 | tf_op jit(solution)/shard_map/ppermute | solution.py:17
  136.0 7.0 %fusion.95 = (f32[2,32,16,256]{3,2,1,0:T(8,128)}, f32[2,32,16,256]{3,2,1,0:T(8,128)S(1)}) fusion(f32[2,32,16,256]{3,2,1,0:T(8,128)S(1)} %constant_dynamic-update-slice_fusion, f32[32,16,256]{2,1,0:T(8,128)} %copy.109, pred[256]{0:T(512)(128)(4,1)S(1)} %copy-done.16, f32[32,16,256]{2,1,0:T(8,128)} %copy.108, f32[2,40,20,256]{3,2,1,0:T(8,128)} %get-tuple-element.41, ...), kind=kLoop, calls=%fused_computation.162 | loop fusion | flops 7340032 | bytes 11534608 | tf_op jit(solution)/shard_map/jit(_where)/select_n | solution.py:60
  146.0 6.0 %collective-permute-start.8 = (f32[2,32,4,256]{3,2,1,0:T(4,128)S(1)}, f32[2,32,4,256]{3,2,1,0:T(4,128)}, u32[]{:S(2)}, u32[]{:S(2)}) collective-permute-start(f32[2,32,4,256]{3,2,1,0:T(4,128)S(1)} %get-tuple-element.44), channel_id=1, source_target_pairs={{0,1},{1,2},{2,3},{4,5},{5,6},{6,7},{8,9},{9,10},{10,11},{12,13},{... | collective-permute-start | bytes 786440 | tf_op jit(solution)/shard_map/ppermute | solution.py:17
  153.7 3.2 %copy.104 = f32[32,16,256]{2,1,0:T(8,128)} copy(f32[32,16,256]{0,2,1:T(8,128)} %fusion.2) | data formatting | bytes 1048576 | tf_op jit(solution)/shard_map/mul | solution.py:160
  158.3 4.3 %collective-permute-done.9 = f32[2,32,4,256]{3,2,1,0:T(4,128)} collective-permute-done((f32[2,32,4,256]{3,2,1,0:T(4,128)}, f32[2,32,4,256]{3,2,1,0:T(4,128)}, u32[]{:S(2)}, u32[]{:S(2)}) %collective-permute-start.9) | collective-permute-done | bytes 262176 | tf_op jit(solution)/shard_map/ppermute | solution.py:18
  163.3 9.4 %fusion.14 = f32[2,32,16,256]{3,2,1,0:T(8,128)S(1)} fusion(f32[2,32,16,256]{3,2,1,0:T(8,128)} %copy-done.6, f32[2,4,16,256]{3,2,1,0:T(8,128)} %collective-permute-done.4, f32[2,32,16,256]{3,2,1,0:T(8,128)S(1)} %copy-done.5, f32[2,4,16,256]{3,2,1,0:T(8,128)} %collective-permute-done.3, f32[2,32,4,256]{3,2,1,0:T(4,128)} %collective-permute-done.9, ...), kind=kLoop, calls=%fused_computation.71 | loop fusion | flops 13107200 | bytes 5505024 | tf_op jit(solution)/shard_map/mul | solution.py:160
  175.5 2.9 %fusion.98 = (f32[32,16,256]{2,1,0:T(8,128)}, f32[32,16,256]{2,1,0:T(8,128)S(1)}) fusion(f32[32,16,256]{2,1,0:T(8,128)S(1)} %scatter-add.12, f32[1,32,16,256]{3,2,1,0:T(8,128)} %param.17, f32[1,32,16,256]{3,2,1,0:T(8,128)} %param.16, f32[32,16,256]{2,1,0:T(8,128)} %copy.110, f32[1,32,16,256]{3,2,1,0:T(8,128)S(1)} %copy-done.9, ...), kind=kLoop, calls=%fused_computation.168 | loop fusion | flops 1179648 | bytes 4718592 | tf_op jit(solution)/shard_map/mul | solution.py:165
  187.6 9.9 %all-to-all-start.3 = ((f32[32,32,256]{2,1,0:T(8,128)}), f32[32,32,256]{2,1,0:T(8,128)S(1)}, u32[]{:S(2)}, u32[]{:S(2)}) async-start(f32[32,32,256]{2,1,0:T(8,128)} %scatter_fusion.1), calls=%async_computation.3 | async-start | bytes 2097152 | tf_op jit(solution)/shard_map/all_to_all | solution.py:174
  197.6 16.0 %scatter_fusion = f32[32,16,256]{2,1,0:T(8,128)S(1)} fusion(f32[32,16,256]{2,1,0:T(8,128)S(1)} %get-tuple-element.53, s32[256]{0:T(256)S(1)} %bitcast.104, f32[256]{0:T(256)S(1)} %and_select_fusion.4), kind=kCustom, calls=%fused_computation.4 | custom fusion | flops 256 | bytes 6144 | tf_op jit(solution)/shard_map/scatter-add | solution.py:86
  213.6 12.5 %all-to-all-done.3 = f32[32,32,256]{2,1,0:T(8,128)S(1)} async-done(((f32[32,32,256]{2,1,0:T(8,128)}), f32[32,32,256]{2,1,0:T(8,128)S(1)}, u32[]{:S(2)}, u32[]{:S(2)}) %all-to-all-start.3) | async-done | bytes 1048608 | tf_op jit(solution)/shard_map/all_to_all | solution.py:174
  (109 shorter events, 48.2 us)
Async XLA Ops:
  0.6 21.8 %copy-start = (f32[4,32,256]{2,1,0:T(8,128)S(1)}, f32[4,32,256]{2,1,0:T(8,128)}, u32[]{:S(2)}) copy-start(f32[4,32,256]{2,1,0:T(8,128)} %param.19) | copy-start | bytes 393220
  0.6 22.4 %copy-start.3 = (f32[4,32,256]{2,1,0:T(8,128)S(1)}, f32[4,32,256]{2,1,0:T(8,128)}, u32[]{:S(2)}) copy-start(f32[4,32,256]{2,1,0:T(8,128)} %param.20) | copy-start | bytes 393220
  25.5 37.0 %copy-start.8 = (f32[1,32,16,256]{3,2,1,0:T(8,128)S(1)}, f32[1,32,16,256]{3,2,1,0:T(8,128)}, u32[]{:S(2)}) copy-start(f32[1,32,16,256]{3,2,1,0:T(8,128)} %param.15) | copy-start | bytes 1572868
  56.8 40.4 %all-to-all-start.2 = ((f32[32,32,256]{2,1,0:T(8,128)}), f32[32,32,256]{2,1,0:T(8,128)}, u32[]{:S(2)}, u32[]{:S(2)}) async-start(f32[32,32,256]{2,1,0:T(8,128)} %get-tuple-element.54), calls=%async_computation.2 | async-start | bytes 2097152 | tf_op jit(solution)/shard_map/all_to_all | solution.py:128
  62.7 6.6 %collective-permute-start.1 = (f32[2,4,16,256]{3,2,1,0:T(8,128)S(1)}, f32[2,4,16,256]{3,2,1,0:T(8,128)S(1)}, u32[]{:S(2)}, u32[]{:S(2)}) collective-permute-start(f32[2,4,16,256]{3,2,1,0:T(8,128)S(1)} %get-tuple-element.51), channel_id=1, source_target_pairs={{0,4},{4,8},{8,12},{1,5},{5,9},{9,13},{2,6},{6,10},{10,14},{3,7},{... | collective-permute-start | bytes 393224 | tf_op jit(solution)/shard_map/ppermute | solution.py:17
  64.0 5.8 %collective-permute-start = (f32[2,4,16,256]{3,2,1,0:T(8,128)S(1)}, f32[2,4,16,256]{3,2,1,0:T(8,128)S(1)}, u32[]{:S(2)}, u32[]{:S(2)}) collective-permute-start(f32[2,4,16,256]{3,2,1,0:T(8,128)S(1)} %get-tuple-element.50), channel_id=1, source_target_pairs={{4,0},{8,4},{12,8},{5,1},{9,5},{13,9},{6,2},{10,6},{14,10},{7,3},{... | collective-permute-start | bytes 393224 | tf_op jit(solution)/shard_map/ppermute | solution.py:18
  66.0 13.5 %copy-start.20 = (s32[16]{0:T(128)}, s32[16]{0:T(128)S(1)}, u32[]{:S(2)}) copy-start(s32[16]{0:T(128)S(1)} %fusion.112) | copy-start | bytes 196
  66.5 16.1 %copy-start.14 = (s32[1024]{0:T(1024)}, s32[1024]{0:T(1024)S(1)}, u32[]{:S(2)}) copy-start(s32[1024]{0:T(1024)S(1)} %pad_clamp_fusion) | copy-start | bytes 12292
  70.8 23.0 %collective-permute-start.5 = (f32[2,40,4,256]{3,2,1,0:T(4,128)}, f32[2,40,4,256]{3,2,1,0:T(4,128)}, u32[]{:S(2)}, u32[]{:S(2)}) collective-permute-start(f32[2,40,4,256]{3,2,1,0:T(4,128)} %get-tuple-element.42), channel_id=1, source_target_pairs={{1,0},{2,1},{3,2},{5,4},{6,5},{7,6},{9,8},{10,9},{11,10},{13,12},{... | collective-permute-start | bytes 983048 | tf_op jit(solution)/shard_map/ppermute | solution.py:18
  72.7 21.1 %collective-permute-start.6 = (f32[2,40,4,256]{3,2,1,0:T(4,128)}, f32[2,40,4,256]{3,2,1,0:T(4,128)}, u32[]{:S(2)}, u32[]{:S(2)}) collective-permute-start(f32[2,40,4,256]{3,2,1,0:T(4,128)} %get-tuple-element.43), channel_id=1, source_target_pairs={{0,1},{1,2},{2,3},{4,5},{5,6},{6,7},{8,9},{9,10},{10,11},{12,13},{... | collective-permute-start | bytes 983048 | tf_op jit(solution)/shard_map/ppermute | solution.py:17
  89.8 16.2 %collective-permute-start.2 = (f32[16,256]{1,0:T(8,128)}, f32[16,256]{1,0:T(8,128)S(1)}, u32[]{:S(2)}, u32[]{:S(2)}) collective-permute-start(f32[16,256]{1,0:T(8,128)} %squeeze.38), channel_id=1, source_target_pairs={{4,0},{8,4},{12,8},{5,1},{9,5},{13,9},{6,2},{10,6},{14,10},{7,3},{... | collective-permute-start | bytes 49160 | tf_op jit(solution)/shard_map/ppermute | solution.py:26
  91.8 16.3 %collective-permute-start.7 = (f32[32,256]{0,1:T(8,128)}, f32[32,256]{0,1:T(8,128)}, u32[]{:S(2)}, u32[]{:S(2)}) collective-permute-start(f32[32,256]{0,1:T(8,128)} %slice_bitcast_fusion.1), channel_id=1, source_target_pairs={{1,0},{2,1},{3,2},{5,4},{6,5},{7,6},{9,8},{10,9},{11,10},{13,12},{... | collective-permute-start | bytes 98312 | tf_op jit(solution)/shard_map/ppermute | solution.py:26
  121.5 36.8 %collective-permute-start.4 = (f32[2,4,16,256]{3,2,1,0:T(8,128)}, f32[2,4,16,256]{3,2,1,0:T(8,128)}, u32[]{:S(2)}, u32[]{:S(2)}) collective-permute-start(f32[2,4,16,256]{3,2,1,0:T(8,128)} %get-tuple-element.49), channel_id=1, source_target_pairs={{4,0},{8,4},{12,8},{5,1},{9,5},{13,9},{6,2},{10,6},{14,10},{7,3},{... | collective-permute-start | bytes 393224 | tf_op jit(solution)/shard_map/ppermute | solution.py:18
  122.8 13.2 %copy-start.16 = (pred[256]{0:T(512)(128)(4,1)S(1)}, pred[256]{0:T(512)(128)(4,1)}, u32[]{:S(2)}) copy-start(pred[256]{0:T(512)(128)(4,1)} %iota_compare_fusion.2) | copy-start | bytes 772
  122.8 13.2 %copy-start.18 = (pred[16]{0:T(512)(128)(4,1)S(1)}, pred[16]{0:T(512)(128)(4,1)}, u32[]{:S(2)}) copy-start(pred[16]{0:T(512)(128)(4,1)} %compare_and_fusion) | copy-start | bytes 52
  128.9 29.4 %collective-permute-start.3 = (f32[2,4,16,256]{3,2,1,0:T(8,128)}, f32[2,4,16,256]{3,2,1,0:T(8,128)}, u32[]{:S(2)}, u32[]{:S(2)}) collective-permute-start(f32[2,4,16,256]{3,2,1,0:T(8,128)} %get-tuple-element.48), channel_id=1, source_target_pairs={{0,4},{4,8},{8,12},{1,5},{5,9},{9,13},{2,6},{6,10},{10,14},{3,7},{... | collective-permute-start | bytes 393224 | tf_op jit(solution)/shard_map/ppermute | solution.py:17
  136.0 16.0 %copy-start.1 = (f32[32,16,16,16]{0,3,2,1:T(8,128)S(1)}, f32[32,16,16,16]{0,3,2,1:T(8,128)}, u32[]{:S(2)}) copy-start(f32[32,16,16,16]{0,3,2,1:T(8,128)} %copy.103) | copy-start | bytes 1572868
  143.9 18.8 %collective-permute-start.9 = (f32[2,32,4,256]{3,2,1,0:T(4,128)}, f32[2,32,4,256]{3,2,1,0:T(4,128)}, u32[]{:S(2)}, u32[]{:S(2)}) collective-permute-start(f32[2,32,4,256]{3,2,1,0:T(4,128)} %get-tuple-element.45), channel_id=1, source_target_pairs={{1,0},{2,1},{3,2},{5,4},{6,5},{7,6},{9,8},{10,9},{11,10},{13,12},{... | collective-permute-start | bytes 786440 | tf_op jit(solution)/shard_map/ppermute | solution.py:18
  146.0 17.3 %collective-permute-start.8 = (f32[2,32,4,256]{3,2,1,0:T(4,128)S(1)}, f32[2,32,4,256]{3,2,1,0:T(4,128)}, u32[]{:S(2)}, u32[]{:S(2)}) collective-permute-start(f32[2,32,4,256]{3,2,1,0:T(4,128)S(1)} %get-tuple-element.44), channel_id=1, source_target_pairs={{0,1},{1,2},{2,3},{4,5},{5,6},{6,7},{8,9},{9,10},{10,11},{12,13},{... | collective-permute-start | bytes 786440 | tf_op jit(solution)/shard_map/ppermute | solution.py:17
  185.0 12.5 %copy-start.22 = (f32[1,256]{1,0:T(1,128)S(1)}, f32[1,256]{1,0:T(1,128)}, u32[]{:S(2)}) copy-start(f32[1,256]{1,0:T(1,128)} %param.27) | copy-start | bytes 3076
  187.6 38.5 %copy-start.13 = (f32[4,32,256]{2,1,0:T(8,128)S(1)}, f32[4,32,256]{2,1,0:T(8,128)}, u32[]{:S(2)}) copy-start(f32[4,32,256]{2,1,0:T(8,128)} %param.21) | copy-start | bytes 393220
  187.6 38.5 %copy-start.19 = (s32[32]{0:T(128)S(1)}, s32[32]{0:T(128)}, u32[]{:S(2)}) copy-start(s32[32]{0:T(128)} %get-tuple-element.33) | copy-start | bytes 388
  187.6 38.5 %all-to-all-start.3 = ((f32[32,32,256]{2,1,0:T(8,128)}), f32[32,32,256]{2,1,0:T(8,128)S(1)}, u32[]{:S(2)}, u32[]{:S(2)}) async-start(f32[32,32,256]{2,1,0:T(8,128)} %scatter_fusion.1), calls=%async_computation.3 | async-start | bytes 2097152 | tf_op jit(solution)/shard_map/all_to_all | solution.py:174
  213.5 14.3 %copy-start.7 = (f32[32,16,256]{2,1,0:T(8,128)}, f32[32,16,256]{2,1,0:T(8,128)S(1)}, u32[]{:S(2)}) copy-start(f32[32,16,256]{2,1,0:T(8,128)S(1)} %scatter_fusion) | copy-start | bytes 1572868
  (12 other events, 81.0 us)
where the time goes:
time: 229 us; the launch traced here: 228 us
  other arithmetic  57.7 us (25%)
  blocking collectives  49.8 us (22%)
  local copies, waits for them, and re-layouts  49.7 us (22%)
  starting transfers between devices  46.6 us (20%)
  waiting for transfers between devices  17.9 us (8%)
  between operations  5.06 us (2%)
    all_to_all x1, blocking collectives, shards(): lax.all_to_all(outgoing[1], 'shot', split_axis=0, concat_axis=0, tiled=True)  31.2 us
    ppermute x4, starting transfers between devices, with_halo(): before = lax.ppermute(last, axis, up)  21.2 us
    all_to_all x1, blocking collectives, shards(): lax.all_to_all(request[:, None], 'shot', split_axis=0, concat_axis=0, til...  18.6 us
    scatter-add x1, other arithmetic, place(): field.at[jnp.clip(loc_x, 0, rows_x - 1), jnp.clip(loc_y, 0, rows_y - 1),...  16 us
    all_to_all x1, waiting for transfers between devices, shards(): lax.all_to_all(sending, 'shot', split_axis=0, concat_axis=0, tiled=True)  12.5 us
    mul x2, other arithmetic, shards(): update = COURANT2 * (dens * vel * vel) * lap  11 us
    all_to_all x1, starting transfers between devices, shards(): lax.all_to_all(sending, 'shot', split_axis=0, concat_axis=0, tiled=True)  9.9 us
    select_n x2, other arithmetic, face_flux(): return jnp.where(inside, 2.0 * forward / safe, 0.0)  9.89 us
  transfers between devices with their start and end apart: 12, of which 4 were waited for; matrix products, arithmetic and copies ran while one was open for 29% of the time, Pallas kernels for 0%

commit v1 on v0

v1 whole, which is shorter than its diff:
```python
import functools

import jax
import jax.numpy as jnp
from jax import lax
from jax.experimental import pallas as pl
from jax.experimental.pallas import tpu as pltpu
from jax.sharding import PartitionSpec as P

COEFS = (1225.0 / 1024.0, -245.0 / 3072.0, 49.0 / 5120.0, -5.0 / 7168.0)
COURANT2 = 0.01
MESH = pl.DeviceIdType.MESH
HIGHEST = lax.Precision.HIGHEST

LX, LY, LZ = 32, 16, 256
NY, NX = 8, 4
NPX, NPY = 4, 4
BLOCKS, HELD, BZ = 16, 4, 16
H = 8


def dot(a, b):
    return jnp.dot(a, b, precision=HIGHEST, preferred_element_type=jnp.float32)


def band(delta, pairs):
    total = jnp.zeros(delta.shape, jnp.float32)
    for offset, weight in pairs:
        total = jnp.where(delta == offset, jnp.float32(weight), total)
    return total


FORWARD = tuple((r, c) for r, c in enumerate(COEFS, 1)) + tuple((1 - r, -c) for r, c in enumerate(COEFS, 1))
BACKWARD = tuple((r - 1, c) for r, c in enumerate(COEFS, 1)) + tuple((-r, -c) for r, c in enumerate(COEFS, 1))


def swap_groups(tiles):
    lane = lax.broadcasted_iota(jnp.int32, (8, 128), 1)
    tiles = [list(t) for t in tiles]
    for a in range(8):
        tiles[a][1], tiles[a + 8][0] = tiles[a + 8][0], tiles[a][1]
    for k in (4, 2, 1):
        set_bit = ((lane >> 4) & k) != 0
        for a in range(16):
            if a & k:
                continue
            for half in range(2):
                low, high = tiles[a][half], tiles[a + k][half]
                tiles[a][half] = jnp.where(set_bit, pltpu.roll(high, 16 * k, 1), low)
                tiles[a + k][half] = jnp.where(set_bit, high, pltpu.roll(low, 128 - 16 * k, 1))
    return tiles


def kernel(
    fwd_now, adj_now, fwd_next, adj_next, velocity, density, gradient_in,
    home_v, home_s, col_s, src_cell, src_amp, rec_cell, rec_val,
    fwd_out, adj_out, grad_out,
    u, nx, fx, fy, fz, lap, rho, vel,
    bd0, bd1, bd2, bd3, bd4, bd5, bd6, bd7,
    bv0, bv1, bv2, bv3, bv4, bv5, bv6, bv7,
    std, stv, gotd, gotv, tmp, sy, hy,
    contrib, gst, grecv,
    p0, p1, p2, p3, p4, p5, p6, p7, rs,
    dz, dzb, my, myb,
    tbl_v, tbl_s, colbuf, colrecv, cols_s,
    loc_sem, agd_s, agd_r, agv_s, agv_r, xd_s, xd_r, xv_s, xv_r, xg_s, xg_r,
    rs_s, rs_r, uh_s, uh_r, dh_s, dh_r, col_ss, col_rs, out_sem,
):
    bd = (bd0, bd1, bd2, bd3, bd4, bd5, bd6, bd7)
    bv = (bv0, bv1, bv2, bv3, bv4, bv5, bv6, bv7)
    part = (p0, p1, p2, p3, p4, p5, p6, p7)
    shot = lax.axis_index("shot")
    px = lax.axis_index("px")
    py = lax.axis_index("py")
    gx = lax.rem(shot, NX)
    gy = shot // NX

    def along_x(e):
        return {"shot": gy * NX + lax.rem(gx + e, NX)}

    def along_y(e):
        return {"shot": lax.rem(gy + e, NY) * NX + gx}

    loads = [
        pltpu.make_async_copy(density, bd0, loc_sem.at[0]),
        pltpu.make_async_copy(fwd_now, u.at[0, pl.ds(H, LX), pl.ds(H, LY), :], loc_sem.at[1]),
        pltpu.make_async_copy(adj_now, u.at[1, pl.ds(H, LX), pl.ds(H, LY), :], loc_sem.at[2]),
        pltpu.make_async_copy(fwd_next, nx.at[0], loc_sem.at[3]),
        pltpu.make_async_copy(adj_next, nx.at[1], loc_sem.at[4]),
        pltpu.make_async_copy(velocity, bv0, loc_sem.at[5]),
        pltpu.make_async_copy(gradient_in, rs.at[8], loc_sem.at[6]),
    ]
    for c in loads:
        c.start()

    def fill(i, _):
        rho[i] = jnp.ones((LY + 2 * H, LZ), jnp.float32)
        return 0

    lax.fori_loop(0, LX + 2 * H, fill, 0)

    def zero_rows(start):
        def body(i, _):
            u[0, H + i, start : start + H, :] = jnp.zeros((H, LZ), jnp.float32)
            u[1, H + i, start : start + H, :] = jnp.zeros((H, LZ), jnp.float32)
            return 0

        lax.fori_loop(0, LX, body, 0)

    def zero_slabs(start):
        def body(i, _):
            u[0, start + i, H : H + LY, :] = jnp.zeros((LY, LZ), jnp.float32)
            u[1, start + i, H : H + LY, :] = jnp.zeros((LY, LZ), jnp.float32)
            return 0

        lax.fori_loop(0, H, body, 0)

    pl.when(py == 0)(lambda: zero_rows(0))
    pl.when(py == NPY - 1)(lambda: zero_rows(H + LY))
    pl.when(px == 0)(lambda: zero_slabs(0))
    pl.when(px == NPX - 1)(lambda: zero_slabs(H + LX))

    barrier = pltpu.get_barrier_semaphore()
    for target in [along_y(1), along_y(NY - 1)] + [along_x(e) for e in range(1, NX)]:
        pl.semaphore_signal(barrier, inc=1, device_id=target, device_id_type=MESH)
    sides = {
        "px_up": (px < NPX - 1, px > 0, {"px": px + 1}),
        "px_down": (px > 0, px < NPX - 1, {"px": px - 1}),
        "py_up": (py < NPY - 1, py > 0, {"py": py + 1}),
        "py_down": (py > 0, py < NPY - 1, {"py": py - 1}),
    }
    for has, _, target in sides.values():

        @pl.when(has)
        def _():
            pl.semaphore_signal(barrier, inc=1, device_id=target, device_id_type=MESH)

    lane8 = lax.broadcasted_iota(jnp.int32, (8, 128), 1)
    within = jnp.zeros((8, 128), jnp.int32)
    depth_of = jnp.zeros((8, 128), jnp.int32)
    for m in range(BLOCKS):
        h = home_v[:, m : m + 1]
        hit = (h >> 2) == lane8
        within = jnp.where(hit, (h & 3) + 1, within)
        depth_of = jnp.where(hit, m, depth_of)
    tbl_v[0] = within
    tbl_v[1] = depth_of
    table_copy = pltpu.make_async_copy(tbl_v, tbl_s, loc_sem.at[7])
    table_copy.start()
    my_col = col_s[0]
    colbuf[...] = jnp.zeros((8, 128), jnp.int32) + my_col

    present = [jnp.where(has, 1, 0) for has, _, _ in sides.values()]
    pl.semaphore_wait(barrier, NX + 1 + sum(present))

    def remote(src, dst, ss, rr, target):
        return pltpu.make_async_remote_copy(
            src_ref=src, dst_ref=dst, send_sem=ss, recv_sem=rr, device_id=target, device_id_type=MESH
        )

    col_copies = [
        remote(colbuf, colrecv.at[e - 1], col_ss.at[e - 1], col_rs.at[e - 1], along_x(e)) for e in range(1, NX)
    ]
    for c in col_copies:
        c.start()

    up, down = along_y(1), along_y(NY - 1)

    def gather(own, b, ss, rr):
        return {
            1: remote(own, b[1], ss.at[1], rr.at[1], up),
            7: remote(own, b[7], ss.at[7], rr.at[7], down),
            2: remote(b[1], b[2], ss.at[2], rr.at[2], up),
            6: remote(b[7], b[6], ss.at[6], rr.at[6], down),
            3: remote(b[2], b[3], ss.at[3], rr.at[3], up),
            5: remote(b[6], b[5], ss.at[5], rr.at[5], down),
            4: remote(b[3].at[pl.ds(0, 2)], b[4].at[pl.ds(0, 2)], ss.at[4], rr.at[4], up),
            0: remote(b[5].at[pl.ds(2, 2)], b[4].at[pl.ds(2, 2)], ss.at[0], rr.at[0], down),
        }

    agd = gather(density, bd, agd_s, agd_r)
    agv = gather(velocity, bv, agv_s, agv_r)
    agd[1].start()
    agd[7].start()

    def halo(f, field):
        s, r = uh_s, uh_r
        return {
            "py_up": remote(field.at[:, pl.ds(LY - H, H), :], u.at[f, pl.ds(H, LX), pl.ds(0, H), :], s.at[f, 0], r.at[f, 0], sides["py_up"][2]),
            "py_down": remote(field.at[:, pl.ds(0, H), :], u.at[f, pl.ds(H, LX), pl.ds(H + LY, H), :], s.at[f, 1], r.at[f, 1], sides["py_down"][2]),
            "px_up": remote(field.at[pl.ds(LX - H, H)], u.at[f, pl.ds(0, H), pl.ds(H, LY), :], s.at[f, 2], r.at[f, 2], sides["px_up"][2]),
            "px_down": remote(field.at[pl.ds(0, H)], u.at[f, pl.ds(H + LX, H), pl.ds(H, LY), :], s.at[f, 3], r.at[f, 3], sides["px_down"][2]),
        }

    def start_sides(copies):
        for name, c in copies.items():
            pl.when(sides[name][0])(c.start)

    def wait_sides(copies):
        for name, c in copies.items():
            pl.when(sides[name][1])(c.wait_recv)

    def finish_sides(copies):
        for name, c in copies.items():
            pl.when(sides[name][0])(c.wait_send)

    halos = [halo(0, fwd_now), halo(1, adj_now)]
    start_sides(halos[0])
    start_sides(halos[1])

    for c in col_copies:
        c.wait_recv()
    cols_copy = pltpu.make_async_copy(colrecv, cols_s, loc_sem.at[8])
    cols_copy.start()
    table_copy.wait()
    cols_copy.wait()
    cols = [my_col] + [cols_s[NX - j - 1, 0, 0] for j in range(1, NX)]

    def owner_at(d):
        return lax.rem(gy + NY - d, NY) * NX + gx

    def within_of(j, d):
        return tbl_s[0, cols[j], owner_at(d)]

    def serve(b, stage, got, ss, rr, d):
        out = []
        for e in range(1, NX):
            stage[e - 1, d] = b[d][jnp.maximum(within_of(e, d) - 1, 0)]
            c = remote(stage.at[e - 1, d], got.at[e * NY + d], ss.at[e - 1, d], rr.at[e - 1, d], along_x(e))
            c.start()
            out.append(c)
        got[d] = b[d][jnp.maximum(within_of(0, d) - 1, 0)]
        return out

    xd, xv = [], []

    def serve_d(*slots):
        for d in slots:
            xd.extend(serve(bd, std, gotd, xd_s, xd_r, d))

    def serve_v(*slots):
        for d in slots:
            xv.extend(serve(bv, stv, gotv, xv_s, xv_r, d))

    def place_of(m):
        owner = home_s[my_col, m] >> 2
        return ((gx - (owner & 3)) & 3) * NY + ((gy - (owner >> 2)) & 7)

    loads[0].wait()
    serve_d(0)

    def build(i, _):
        start = pl.multiple_of(i * 32, 32)
        row = lax.broadcasted_iota(jnp.int32, (32, 256), 0) + start
        colm = lax.broadcasted_iota(jnp.int32, (32, 256), 1)
        forward = jnp.where(colm < LZ - 1, band(row - colm, FORWARD), 0.0)
        dz[pl.ds(start, 32), :] = forward
        dzb[pl.ds(start, 32), :] = band(row - colm, BACKWARD)
        same = (row >> 5) == (colm >> 5)
        my[pl.ds(start, 32), :] = jnp.where(same, band(colm - row, FORWARD), 0.0)
        return 0

    lax.fori_loop(0, 8, build, 0)

    def build_back(i, _):
        start = pl.multiple_of(i * 32, 32)
        row = lax.broadcasted_iota(jnp.int32, (32, 256), 0) + start
        colm = lax.broadcasted_iota(jnp.int32, (32, 256), 1)
        same = (row >> 4) == (colm >> 5)
        delta = ((colm & 31) - H) - (row & 15)
        myb[pl.ds(start, 32), :] = jnp.where(same, band(delta, BACKWARD), 0.0)
        return 0

    lax.fori_loop(0, 4, build_back, 0)

    agd[1].wait_recv()
    agd[2].start()
    agd[7].wait_recv()
    agd[6].start()
    serve_d(1, 7)

    loads[1].wait()
    loads[2].wait()

    def forward_z(f):
        def body(g, _):
            block = u[f, pl.ds(H + 8 * g, 8), H : H + LY, :].reshape(8 * LY, LZ)
            fz[f, pl.ds(8 * g, 8)] = dot(block, dz[...]).reshape(8, LY, LZ)
            return 0

        lax.fori_loop(0, 4, body, 0)

    forward_z(0)
    agd[2].wait_recv()
    agd[3].start()
    agd[6].wait_recv()
    agd[5].start()
    serve_d(2, 6)
    forward_z(1)

    agd[3].wait_recv()
    agd[4].start()
    agd[5].wait_recv()
    agd[0].start()
    agv[1].start()
    agv[7].start()
    serve_d(3, 5)

    cell = rec_cell[...]
    cell_x = (cell >> 14) - px * LX
    cell_y = ((cell >> 8) & 63) - py * LY
    cell_z = cell & 255
    here = (cell_x >= 0) & (cell_x < LX) & (cell_y >= 0) & (cell_y < LY)
    spot = jnp.where(here, cell_x * LY + cell_y, -1)
    by_depth = jnp.where(lax.broadcasted_iota(jnp.int32, (LZ, 256), 0) == cell_z, rec_val[...], 0.0)
    loads[3].wait()
    loads[4].wait()

    def bases(g, _):
        start = pl.multiple_of(g * 128, 128)
        at = (lax.broadcasted_iota(jnp.int32, (128, 256), 0) + start == spot).astype(jnp.float32)
        added = lax.dot_general(
            at, by_depth, (((1,), (1,)), ((), ())), precision=HIGHEST, preferred_element_type=jnp.float32
        ).reshape(8, LY, LZ)
        rows = pl.ds(8 * g, 8)
        nx[0, rows] = 2.0 * u[0, pl.ds(H + 8 * g, 8), H : H + LY, :] - nx[0, rows]
        nx[1, rows] = 2.0 * u[1, pl.ds(H + 8 * g, 8), H : H + LY, :] - nx[1, rows] + added
        return 0

    lax.fori_loop(0, 4, bases, 0)

    agd[4].wait_recv()
    agd[0].wait_recv()
    serve_d(4)
    loads[5].wait()
    serve_v(0)

    def forward_xy(f):
        def body_x(k, _):
            total = None
            for r, weight in enumerate(COEFS, 1):
                term = weight * (u[f, k + 4 + r, H : H + LY, :] - u[f, k + 5 - r, H : H + LY, :])
                total = term if total is None else total + term
            fx[f, k] = total
            return 0

        lax.fori_loop(0, LX + 7, body_x, 0)

        def body_y(g, _):
            block = u[f, pl.ds(H + 8 * g, 8)].reshape(8 * (LY + 2 * H), LZ)
            fy[f, pl.ds(8 * g, 8)] = dot(my[...], block).reshape(8, LY + 2 * H, LZ)
            return 0

        lax.fori_loop(0, 4, body_y, 0)

    wait_sides(halos[0])
    forward_xy(0)

    agv[1].wait_recv()
    agv[2].start()
    agv[7].wait_recv()
    agv[6].start()
    serve_v(1, 7)

    def to_pencil(got, store):
        places = [place_of(m) for m in range(BLOCKS)]

        def body(g, _):
            tiles = []
            for m in range(BLOCKS):
                slab = got[places[m], pl.ds(pl.multiple_of(8 * g, 8), 8), :]
                tiles.append([slab[:, :128], slab[:, 128:]])
            tiles = swap_groups(tiles)
            for y in range(LY):
                for half in range(2):
                    tmp[half, pl.ds(g * 128 + y, 8, stride=16), :] = tiles[y][half]
            for half in range(2):
                rows = tmp[half, pl.ds(pl.multiple_of(g * 128, 128), 128), :]
                store(g, half, rows.reshape(8, LY, 128))
            return 0

        lax.fori_loop(0, 4, body, 0)

    def store_rho(g, half, value):
        rho[pl.ds(H + 8 * g, 8), H : H + LY, half * 128 : half * 128 + 128] = value

    def store_vel(g, half, value):
        vel[pl.ds(8 * g, 8), :, half * 128 : half * 128 + 128] = value

    for c in xd:
        c.wait_recv()
    to_pencil(gotd, store_rho)

    def pack(i, _):
        sy[0, i, 0:4, :] = rho[H + i, H + 12 : H + 16, :]
        sy[0, i, 4:8, :] = rho[H + 16 + i, H + 12 : H + 16, :]
        sy[1, i, 0:4, :] = rho[H + i, H : H + 4, :]
        sy[1, i, 4:8, :] = rho[H + 16 + i, H : H + 4, :]
        return 0

    lax.fori_loop(0, 16, pack, 0)
    rho_halo = {
        "py_up": remote(sy.at[0], hy.at[0], dh_s.at[0], dh_r.at[0], sides["py_up"][2]),
        "py_down": remote(sy.at[1], hy.at[1], dh_s.at[1], dh_r.at[1], sides["py_down"][2]),
        "px_up": remote(rho.at[pl.ds(H + LX - 4, 4), pl.ds(H, LY), :], rho.at[pl.ds(H - 4, 4), pl.ds(H, LY), :], dh_s.at[2], dh_r.at[2], sides["px_up"][2]),
        "px_down": remote(rho.at[pl.ds(H, 4), pl.ds(H, LY), :], rho.at[pl.ds(H + LX, 4), pl.ds(H, LY), :], dh_s.at[3], dh_r.at[3], sides["px_down"][2]),
    }
    start_sides(rho_halo)

    agv[2].wait_recv()
    agv[3].start()
    agv[6].wait_recv()
    agv[5].start()
    serve_v(2, 6)

    def depth_part(g, _):
        block = rho[pl.ds(H + 8 * g, 8), H : H + LY, :].reshape(8 * LY, LZ)
        scale = 2.0 / (block + pltpu.roll(block, LZ - 1, 1))
        rows = pl.ds(8 * g, 8)
        for f in range(2):
            flux = fz[f, rows].reshape(8 * LY, LZ) * scale
            lap[f, rows] = dot(flux, dzb[...]).reshape(8, LY, LZ)
        return 0

    lax.fori_loop(0, 4, depth_part, 0)

    agv[3].wait_recv()
    agv[4].start()
    agv[5].wait_recv()
    agv[0].start()
    serve_v(3, 5)

    wait_sides(halos[1])
    forward_xy(1)

    agv[4].wait_recv()
    agv[0].wait_recv()
    serve_v(4)

    wait_sides(rho_halo)

    @pl.when(py > 0)
    def _():
        def body(i, _):
            rho[H + i, H - 4 : H, :] = hy[0, i, 0:4, :]
            rho[H + 16 + i, H - 4 : H, :] = hy[0, i, 4:8, :]
            return 0

        lax.fori_loop(0, 16, body, 0)

    @pl.when(py < NPY - 1)
    def _():
        def body(i, _):
            rho[H + i, H + LY : H + LY + 4, :] = hy[1, i, 0:4, :]
            rho[H + 16 + i, H + LY : H + LY + 4, :] = hy[1, i, 4:8, :]
            return 0

        lax.fori_loop(0, 16, body, 0)

    def flux_x(k, _):
        face = px * LX + k - 4
        two = jnp.where((face >= 0) & (face <= NPX * LX - 2), 2.0, 0.0)
        scale = two / (rho[k + 4, H : H + LY, :] + rho[k + 5, H : H + LY, :])
        for f in range(2):
            fx[f, k] = fx[f, k] * scale
        return 0

    lax.fori_loop(0, LX + 7, flux_x, 0)

    rows_y = lax.broadcasted_iota(jnp.int32, (LY + 2 * H, LZ), 0) - H
    face_y = rows_y + py * LY
    open_y = (rows_y >= -4) & (rows_y < LY + 3) & (face_y >= 0) & (face_y <= NPY * LY - 2)

    def flux_y(i, _):
        line = rho[H + i]
        scale = jnp.where(open_y, 2.0 / (line + pltpu.roll(line, LY + 2 * H - 1, 0)), 0.0)
        for f in range(2):
            fy[f, i] = fy[f, i] * scale
        return 0

    lax.fori_loop(0, LX, flux_y, 0)

    def laplacian(f, g):
        block = fy[f, pl.ds(8 * g, 8)].reshape(8 * (LY + 2 * H), LZ)
        total = lap[f, pl.ds(8 * g, 8)] + dot(myb[...], block).reshape(8, LY, LZ)
        for r, weight in enumerate(COEFS, 1):
            total = total + weight * (fx[f, pl.ds(8 * g + 3 + r, 8)] - fx[f, pl.ds(8 * g + 4 - r, 8)])
        return total

    for c in xv:
        c.wait_recv()
    to_pencil(gotv, store_vel)

    cell_s = src_cell[0]
    amp = src_amp[0]
    shape = (8, LY, LZ)
    iota_x = lax.broadcasted_iota(jnp.int32, shape, 0)
    iota_y = lax.broadcasted_iota(jnp.int32, shape, 1)
    iota_z = lax.broadcasted_iota(jnp.int32, shape, 2)
    flat = ((iota_x + px * LX) * (NPY * LY) + iota_y + py * LY) * LZ + iota_z

    def source_field(g, _):
        rows = pl.ds(8 * g, 8)
        v = vel[rows]
        step = COURANT2 * (rho[pl.ds(H + 8 * g, 8), H : H + LY, :] * v * v) * laplacian(0, g)
        step = step - jnp.where(flat + g * (8 * NPY * LY * LZ) == cell_s, amp, 0.0)
        nx[0, rows] = nx[0, rows] + step
        value = (2.0 / v) * u[1, pl.ds(H + 8 * g, 8), H : H + LY, :] * step
        for half in range(2):
            tmp[half, pl.ds(pl.multiple_of(g * 128, 128), 128), :] = value[:, :, half * 128 : half * 128 + 128].reshape(128, 128)
        tiles = []
        for y in range(LY):
            tiles.append([tmp[half, pl.ds(g * 128 + y, 8, stride=16), :] for half in range(2)])
        tiles = swap_groups(tiles)
        for m in range(BLOCKS):
            for half in range(2):
                contrib[m, pl.ds(pl.multiple_of(8 * g, 8), 8), half * 128 : half * 128 + 128] = tiles[m][half]
        return 0

    lax.fori_loop(0, 4, source_field, 0)
    out_f = pltpu.make_async_copy(nx.at[0], fwd_out, out_sem.at[0])
    out_f.start()

    xg = {}
    for d in (4, 3, 5, 2, 6, 1, 7, 0):
        for e in range(1, NX):
            owner = lax.rem(gy + NY - d, NY) * NX + lax.rem(gx + e, NX)
            gst[e - 1, d] = contrib[tbl_s[1, my_col, owner]]
            c = remote(gst.at[e - 1, d], grecv.at[e - 1, d], xg_s.at[e - 1, d], xg_r.at[e - 1, d], along_x(e))
            c.start()
            xg[e, d] = c

    def adjoint_field(g, _):
        rows = pl.ds(8 * g, 8)
        v = vel[rows]
        step = COURANT2 * (rho[pl.ds(H + 8 * g, 8), H : H + LY, :] * v * v) * laplacian(1, g)
        nx[1, rows] = nx[1, rows] + step
        return 0

    lax.fori_loop(0, 4, adjoint_field, 0)
    out_a = pltpu.make_async_copy(nx.at[1], adj_out, out_sem.at[1])
    out_a.start()

    def collect(d):
        for e in range(1, NX):
            xg[e, d].wait_recv()
        values = [contrib[tbl_s[1, my_col, owner_at(d)]]] + [grecv[NX - j - 1, d] for j in range(1, NX)]
        picks = [within_of(j, d) for j in range(NX)]
        for w in range(HELD):
            total = jnp.zeros((LX, LZ), jnp.float32)
            for j in range(NX):
                total = total + jnp.where(picks[j] == w + 1, values[j], 0.0)
            part[d][w] = total

    halves = (pl.ds(0, 2), pl.ds(2, 2))

    def send(src, slot, sem, target):
        c = remote(src, rs.at[slot], rs_s.at[sem], rs_r.at[sem], target)
        c.start()
        return c

    collect(4)
    m3 = remote(p4.at[halves[0]], rs.at[3, halves[0]], rs_s.at[3], rs_r.at[3], down)
    q5 = remote(p4.at[halves[1]], rs.at[5, halves[1]], rs_s.at[5], rs_r.at[5], up)
    m3.start()
    q5.start()
    collect(3)
    collect(5)
    m3.wait_recv()
    p3[0:2] = p3[0:2] + rs[3, 0:2]
    m2 = send(p3, 2, 2, down)
    q5.wait_recv()
    p5[2:4] = p5[2:4] + rs[5, 2:4]
    q6 = send(p5, 6, 6, up)
    collect(2)
    collect(6)
    m2.wait_recv()
    p2[...] = p2[...] + rs[2]
    m1 = send(p2, 1, 1, down)
    q6.wait_recv()
    p6[...] = p6[...] + rs[6]
    q7 = send(p6, 7, 7, up)
    collect(1)
    collect(7)
    m1.wait_recv()
    p1[...] = p1[...] + rs[1]
    m0 = send(p1, 0, 0, down)
    q7.wait_recv()
    p7[...] = p7[...] + rs[7]
    q0 = send(p7, 4, 4, up)
    collect(0)
    loads[6].wait()
    p0[...] = p0[...] + rs[8]
    m0.wait_recv()
    q0.wait_recv()
    p0[...] = p0[...] + (rs[0] + rs[4])
    out_g = pltpu.make_async_copy(p0, grad_out, out_sem.at[2])
    out_g.start()

    for c in col_copies + xd + xv + list(xg.values()) + list(agd.values()) + list(agv.values()):
        c.wait_send()
    for c in (m3, q5, m2, q6, m1, q7, m0, q0):
        c.wait_send()
    finish_sides(halos[0])
    finish_sides(halos[1])
    finish_sides(rho_halo)
    out_f.wait()
    out_a.wait()
    out_g.wait()


def shards(
    fwd_now,
    fwd_next,
    adj_now,
    adj_next,
    velocity,
    density,
    gradient_in,
    block_home,
    aperture_col,
    source_cell,
    source_amp,
    receiver_cell,
    receiver_residual,
):
    f32, i32 = jnp.float32, jnp.int32
    any_space = pl.BlockSpec(memory_space=pl.ANY)
    vmem = pl.BlockSpec(memory_space=pltpu.VMEM)
    smem = pl.BlockSpec(memory_space=pltpu.SMEM)
    pencil = (LX, LY, LZ)
    blocks = (HELD, LX, LZ)
    V = pltpu.VMEM
    D = pltpu.SemaphoreType.DMA
    scratch = [
        V((2, LX + 2 * H, LY + 2 * H, LZ), f32),
        V((2,) + pencil, f32),
        V((2, LX + 8, LY, LZ), f32),
        V((2, LX, LY + 2 * H, LZ), f32),
        V((2,) + pencil, f32),
        V((2,) + pencil, f32),
        V((LX + 2 * H, LY + 2 * H, LZ), f32),
        V(pencil, f32),
    ]
    scratch += [V(blocks, f32) for _ in range(16)]
    scratch += [
        V((NX - 1, NY, LX, LZ), f32),
        V((NX - 1, NY, LX, LZ), f32),
        V((NX * NY, LX, LZ), f32),
        V((NX * NY, LX, LZ), f32),
        V((2, LX * LY, 128), f32),
        V((2, 16, 8, LZ), f32),
        V((2, 16, 8, LZ), f32),
        V((BLOCKS, LX, LZ), f32),
        V((NX - 1, NY, LX, LZ), f32),
        V((NX - 1, NY, LX, LZ), f32),
    ]
    scratch += [V(blocks, f32) for _ in range(8)]
    scratch += [
        V((9,) + blocks, f32),
        V((256, 256), f32),
        V((256, 256), f32),
        V((256, 256), f32),
        V((128, 256), f32),
        V((2, 8, 128), i32),
        pltpu.SMEM((2, 8, 128), i32),
        V((8, 128), i32),
        V((NX - 1, 8, 128), i32),
        pltpu.SMEM((NX - 1, 8, 128), i32),
        D((9,)),
        D((8,)), D((8,)), D((8,)), D((8,)),
        D((3, 8)), D((3, 8)), D((3, 8)), D((3, 8)), D((3, 8)), D((3, 8)),
        D((8,)), D((8,)),
        D((2, 4)), D((2, 4)),
        D((4,)), D((4,)),
        D((3,)), D((3,)),
        D((3,)),
    ]
    fwd, adj, grad = pl.pallas_call(
        kernel,
        out_shape=(
            jax.ShapeDtypeStruct(pencil, f32),
            jax.ShapeDtypeStruct(pencil, f32),
            jax.ShapeDtypeStruct(blocks, f32),
        ),
        in_specs=[any_space] * 7 + [vmem, smem, smem, smem, smem, vmem, vmem],
        out_specs=(any_space, any_space, any_space),
        scratch_shapes=scratch,
        compiler_params=pltpu.CompilerParams(
            collective_id=0, has_side_effects=True, vmem_limit_bytes=48 * 2**20
        ),
        name="wave_step",
    )(
        fwd_now[0], adj_now[0], fwd_next[0], adj_next[0], velocity, density, gradient_in,
        block_home, block_home, aperture_col, source_cell, source_amp, receiver_cell, receiver_residual,
    )
    return fwd[None], adj[None], grad


def solution(mesh):
    in_specs = (
        P("shot", "px", "py", None),
        P("shot", "px", "py", None),
        P("shot", "px", "py", None),
        P("shot", "px", "py", None),
        P("shot", "px", "py"),
        P("shot", "px", "py"),
        P("shot", "px", "py"),
        P(),
        P("shot"),
        P("shot"),
        P("shot"),
        P("shot", None),
        P("shot", None),
    )
    out_specs = (P("shot", "px", "py", None), P("shot", "px", "py", None), P("shot", "px", "py"))
    return jax.shard_map(shards, mesh=mesh, in_specs=in_specs, out_specs=out_specs, check_vma=False)
```

time: 229 us -> 91 us (0.40)
  the two profiles are of different devices: /device:TPU:130 before, /device:TPU:128 now
where the time goes in v1:
time: 91 us; the launch traced here: 90.6 us
  Pallas kernels  78.2 us (86%)
  local copies, waits for them, and re-layouts  9.81 us (11%)
  between operations  2.61 us (3%)
    pallas_call x1, Pallas kernels, shards(): pl.pallas_call(kernel, out_shape=(jax.ShapeDtypeStruct(pencil, f32), jax....  78.2 us
    unnamed x23, local copies, waits for them, and re-layouts  9.81 us

profile of v1, /device:TPU:128, one launch (start us, length us, event | category | flops | bytes accessed | tf_op | source)
XLA Modules:
  0.0 90.6 jit_solution(12015472252886314055)
XLA Ops:
  2.6 0.0 copy-start.7
  2.6 0.0 copy-start.9
  2.6 0.0 copy-start.8
  2.6 0.7 copy-done.7
  3.3 0.0 copy-done.9
  3.3 0.0 copy-done.8
  3.3 0.0 copy-start
  3.3 1.0 %copy-done = f32[1,32,16,256]{3,2,1,0:T(8,128)S(1)} copy-done((f32[1,32,16,256]{3,2,1,0:T(8,128)S(1)}, f32[1,32,16,256]{3,2,1,0:T(8,128)}, u32[]{:S(2)}) %copy-start) | copy-done | bytes 524312
  4.3 0.0 copy-start.1
  4.3 1.0 %copy-done.1 = f32[1,32,16,256]{3,2,1,0:T(8,128)S(1)} copy-done((f32[1,32,16,256]{3,2,1,0:T(8,128)S(1)}, f32[1,32,16,256]{3,2,1,0:T(8,128)}, u32[]{:S(2)}) %copy-start.1) | copy-done | bytes 524312
  5.4 0.0 copy-start.2
  5.4 1.0 %copy-done.2 = f32[1,32,16,256]{3,2,1,0:T(8,128)S(1)} copy-done((f32[1,32,16,256]{3,2,1,0:T(8,128)S(1)}, f32[1,32,16,256]{3,2,1,0:T(8,128)}, u32[]{:S(2)}) %copy-start.2) | copy-done | bytes 524312
  6.4 0.0 copy-start.3
  6.4 1.0 %copy-done.3 = f32[1,32,16,256]{3,2,1,0:T(8,128)S(1)} copy-done((f32[1,32,16,256]{3,2,1,0:T(8,128)S(1)}, f32[1,32,16,256]{3,2,1,0:T(8,128)}, u32[]{:S(2)}) %copy-start.3) | copy-done | bytes 524312
  7.5 0.0 copy-start.4
  7.5 0.9 copy-done.4
  8.4 0.0 copy-start.5
  8.4 0.9 copy-done.5
  9.3 0.0 copy-start.6
  9.3 0.9 copy-done.6
  10.2 78.2 %wave_step.1 = (f32[32,16,256]{2,1,0:T(8,128)S(1)}, f32[32,16,256]{2,1,0:T(8,128)S(1)}, f32[4,32,256]{2,1,0:T(8,128)S(1)}) custom-call(f32[32,16,256]{2,1,0:T(8,128)S(1)} %bitcast.8, f32[32,16,256]{2,1,0:T(8,128)S(1)} %bitcast.9, f32[32,16,256]{2,1,0:T(8,128)S(1)} %bitcast.10, f32[32,16,256]{2,1,0:T(8,128)S(1)} %bitcast.11, f32[4,32,256]{2,1,0:T(8,128)S(1)} %copy-done.4, ...), custom_call_target="tpu_custom_call" | custom-call | tf_op jit(solution)/shard_map/wave_step/pallas_call | solution.py:679
  88.4 0.8 copy.22
  89.2 0.8 copy.23
  90.0 0.7 copy.24
Async XLA Ops:
  2.6 0.7 copy-start.7
  2.6 0.7 copy-start.9
  2.6 0.7 copy-start.8
  3.3 1.0 %copy-start = (f32[1,32,16,256]{3,2,1,0:T(8,128)S(1)}, f32[1,32,16,256]{3,2,1,0:T(8,128)}, u32[]{:S(2)}) copy-start(f32[1,32,16,256]{3,2,1,0:T(8,128)} %param.13) | copy-start | bytes 1572868
  4.3 1.0 %copy-start.1 = (f32[1,32,16,256]{3,2,1,0:T(8,128)S(1)}, f32[1,32,16,256]{3,2,1,0:T(8,128)}, u32[]{:S(2)}) copy-start(f32[1,32,16,256]{3,2,1,0:T(8,128)} %param.15) | copy-start | bytes 1572868
  5.4 1.0 %copy-start.2 = (f32[1,32,16,256]{3,2,1,0:T(8,128)S(1)}, f32[1,32,16,256]{3,2,1,0:T(8,128)}, u32[]{:S(2)}) copy-start(f32[1,32,16,256]{3,2,1,0:T(8,128)} %param.14) | copy-start | bytes 1572868
  6.4 1.0 %copy-start.3 = (f32[1,32,16,256]{3,2,1,0:T(8,128)S(1)}, f32[1,32,16,256]{3,2,1,0:T(8,128)}, u32[]{:S(2)}) copy-start(f32[1,32,16,256]{3,2,1,0:T(8,128)} %param.16) | copy-start | bytes 1572868
  7.5 0.9 copy-start.4
  8.4 0.9 copy-start.5
  9.3 0.9 copy-start.6

commit v2 on v1

v2 whole, which is shorter than its diff:
```python
import functools

import jax
import jax.numpy as jnp
from jax import lax
from jax.experimental import pallas as pl
from jax.experimental.pallas import tpu as pltpu
from jax.sharding import PartitionSpec as P

COEFS = (1225.0 / 1024.0, -245.0 / 3072.0, 49.0 / 5120.0, -5.0 / 7168.0)
COURANT2 = 0.01
MESH = pl.DeviceIdType.MESH
HIGHEST = lax.Precision.HIGHEST

LX, LY, LZ = 32, 16, 256
NY, NX = 8, 4
NPX, NPY = 4, 4
BLOCKS, HELD, BZ = 16, 4, 16
H = 8


def dot(a, b):
    return jnp.dot(a, b, precision=HIGHEST, preferred_element_type=jnp.float32)


def band(delta, pairs):
    total = jnp.zeros(delta.shape, jnp.float32)
    for offset, weight in pairs:
        total = jnp.where(delta == offset, jnp.float32(weight), total)
    return total


FORWARD = tuple((r, c) for r, c in enumerate(COEFS, 1)) + tuple((1 - r, -c) for r, c in enumerate(COEFS, 1))
BACKWARD = tuple((r - 1, c) for r, c in enumerate(COEFS, 1)) + tuple((-r, -c) for r, c in enumerate(COEFS, 1))


def swap_groups(tiles):
    lane = lax.broadcasted_iota(jnp.int32, (8, 128), 1)
    tiles = [list(t) for t in tiles]
    for a in range(8):
        tiles[a][1], tiles[a + 8][0] = tiles[a + 8][0], tiles[a][1]
    for k in (4, 2, 1):
        set_bit = ((lane >> 4) & k) != 0
        for a in range(16):
            if a & k:
                continue
            for half in range(2):
                low, high = tiles[a][half], tiles[a + k][half]
                tiles[a][half] = jnp.where(set_bit, pltpu.roll(high, 16 * k, 1), low)
                tiles[a + k][half] = jnp.where(set_bit, high, pltpu.roll(low, 128 - 16 * k, 1))
    return tiles


def kernel(
    fwd_now, adj_now, fwd_next, adj_next, velocity, density, gradient_in,
    home, col, source, amplitude, receivers, residuals,
    fwd_out, adj_out, grad_out,
    u, nx, fx, fy, fz, lap, rho, vel,
    std, got0, got1, tmp, sy, hy,
    con, gst, grecv, gin, rs,
    dz, dzb, my, myb,
    tbl_v, tbl_s, colbuf, colrecv, cols_s,
    loc_sem, ag_s, ag_r, xd_s, xd_r, xg_s, xg_r,
    rs_s, rs_r, uh_s, uh_r, dh_s, dh_r, col_ss, col_rs, out_sem,
    home_v, home_s, col_s, src_cell, src_amp, rec_cell, rec_val, small_sem,
    note, notes, spike, nx_s, nx_r, ny_s, ny_r,
    *slots,
):
    chunk = [slots[8 * c : 8 * c + 8] for c in range(2)]
    part = slots[16:24]
    got = (got0, got1)
    place = {0: 0, 1: 1, 7: 2, 2: 3, 6: 4, 3: 5, 5: 6, 4: 7}
    shot = lax.axis_index("shot")
    px = lax.axis_index("px")
    py = lax.axis_index("py")
    gx = lax.rem(shot, NX)
    gy = shot // NX

    def along_x(e):
        return {"shot": gy * NX + lax.rem(gx + e, NX)}

    def along_y(e):
        return {"shot": lax.rem(gy + e, NY) * NX + gx}

    own = (density, velocity)
    own_loads = [pltpu.make_async_copy(own[c], chunk[c][0], loc_sem.at[c]) for c in range(2)]
    loads = [
        pltpu.make_async_copy(fwd_now, u.at[0, pl.ds(H, LX), pl.ds(H, LY), :], loc_sem.at[4]),
        pltpu.make_async_copy(adj_now, u.at[1, pl.ds(H, LX), pl.ds(H, LY), :], loc_sem.at[5]),
        pltpu.make_async_copy(fwd_next, nx.at[0], loc_sem.at[6]),
        pltpu.make_async_copy(adj_next, nx.at[1], loc_sem.at[7]),
        pltpu.make_async_copy(gradient_in, gin, loc_sem.at[8]),
    ]
    small = [
        pltpu.make_async_copy(src, dst, small_sem.at[i])
        for i, (src, dst) in enumerate(
            (
                (col, col_s), (home, home_v), (home, home_s), (source, src_cell),
                (amplitude, src_amp), (receivers, rec_cell), (residuals, rec_val),
            )
        )
    ]
    for c in small + own_loads + loads:
        c.start()

    def zero_rows(start):
        def body(i, _):
            u[0, H + i, start : start + H, :] = jnp.zeros((H, LZ), jnp.float32)
            u[1, H + i, start : start + H, :] = jnp.zeros((H, LZ), jnp.float32)
            return 0

        lax.fori_loop(0, LX, body, 0)

    def zero_slabs(start):
        def body(i, _):
            u[0, start + i, H : H + LY, :] = jnp.zeros((LY, LZ), jnp.float32)
            u[1, start + i, H : H + LY, :] = jnp.zeros((LY, LZ), jnp.float32)
            return 0

        lax.fori_loop(0, H, body, 0)

    barrier = pltpu.get_barrier_semaphore()
    for target in [along_y(1), along_y(NY - 1)] + [along_x(e) for e in range(1, NX)]:
        pl.semaphore_signal(barrier, inc=1, device_id=target, device_id_type=MESH)
    sides = {
        "px_up": (px < NPX - 1, px > 0, {"px": px + 1}),
        "px_down": (px > 0, px < NPX - 1, {"px": px - 1}),
        "py_up": (py < NPY - 1, py > 0, {"py": py + 1}),
        "py_down": (py > 0, py < NPY - 1, {"py": py - 1}),
    }
    for has, _, target in sides.values():

        @pl.when(has)
        def _():
            pl.semaphore_signal(barrier, inc=1, device_id=target, device_id_type=MESH)

    small[0].wait()
    my_col = col_s[0]
    colbuf[...] = jnp.zeros((8, 128), jnp.int32) + my_col

    present = [jnp.where(has, 1, 0) for has, _, _ in sides.values()]
    pl.semaphore_wait(barrier, NX + 1 + sum(present))

    def remote(src, dst, ss, rr, target):
        return pltpu.make_async_remote_copy(
            src_ref=src, dst_ref=dst, send_sem=ss, recv_sem=rr, device_id=target, device_id_type=MESH
        )

    col_copies = [
        remote(colbuf, colrecv.at[e - 1], col_ss.at[e - 1], col_rs.at[e - 1], along_x(e)) for e in range(1, NX)
    ]
    for c in col_copies:
        c.start()

    up, down = along_y(1), along_y(NY - 1)

    halves = (pl.ds(0, 2), pl.ds(2, 2))

    def gather(c):
        b, out = chunk[c], {}
        for d, src, target in (
            (1, own[c], up), (7, own[c], down), (2, b[1], up), (6, b[7], down),
            (3, b[2], up), (5, b[6], down), (4, b[3], up), (4, b[5], down),
        ):
            for w in range(2):
                if d == 4 and w != (0 if target is up else 1):
                    continue
                out[d, w] = remote(src.at[halves[w]], b[d].at[halves[w]], ag_s.at[c, d, w], ag_r.at[c, d, w], target)
        return out

    ag = [gather(c) for c in range(2)]

    def first(c):
        for w in range(2):
            ag[c][1, w].start()
            ag[c][7, w].start()

    def forward(c, d):
        for w in range(2):
            for k, to in ((d, d + 1), (NY - d, NY - d - 1)):
                ag[c][k, w].wait_recv()
                if (to, w) in ag[c] and not (to == 4 and w != (0 if k == 3 else 1)):
                    ag[c][to, w].start()

    first(0)

    def halo(f, field):
        s, r = uh_s, uh_r
        return {
            "py_up": remote(field.at[:, pl.ds(LY - H, H), :], u.at[f, pl.ds(H, LX), pl.ds(0, H), :], s.at[f, 0], r.at[f, 0], sides["py_up"][2]),
            "py_down": remote(field.at[:, pl.ds(0, H), :], u.at[f, pl.ds(H, LX), pl.ds(H + LY, H), :], s.at[f, 1], r.at[f, 1], sides["py_down"][2]),
            "px_up": remote(field.at[pl.ds(LX - H, H)], u.at[f, pl.ds(0, H), pl.ds(H, LY), :], s.at[f, 2], r.at[f, 2], sides["px_up"][2]),
            "px_down": remote(field.at[pl.ds(0, H)], u.at[f, pl.ds(H + LX, H), pl.ds(H, LY), :], s.at[f, 3], r.at[f, 3], sides["px_down"][2]),
        }

    def start_sides(copies):
        for name, c in copies.items():
            pl.when(sides[name][0])(c.start)

    def wait_sides(copies):
        for name, c in copies.items():
            pl.when(sides[name][1])(c.wait_recv)

    def finish_sides(copies):
        for name, c in copies.items():
            pl.when(sides[name][0])(c.wait_send)

    halos = [halo(0, fwd_now), halo(1, adj_now)]
    start_sides(halos[0])
    start_sides(halos[1])
    small[1].wait()
    small[2].wait()
    lane8 = lax.broadcasted_iota(jnp.int32, (8, 128), 1)
    within = jnp.zeros((8, 128), jnp.int32)
    depth_of = jnp.zeros((8, 128), jnp.int32)
    for m in range(BLOCKS):
        h = home_v[:, m : m + 1]
        hit = (h >> 2) == lane8
        within = jnp.where(hit, (h & 3) + 1, within)
        depth_of = jnp.where(hit, m, depth_of)
    tbl_v[0] = within
    tbl_v[1] = depth_of
    table_copy = pltpu.make_async_copy(tbl_v, tbl_s, loc_sem.at[9])
    table_copy.start()
    pl.when(py == 0)(lambda: zero_rows(0))
    pl.when(py == NPY - 1)(lambda: zero_rows(H + LY))
    pl.when(px == 0)(lambda: zero_slabs(0))
    pl.when(px == NPX - 1)(lambda: zero_slabs(H + LX))

    for c in col_copies:
        c.wait_recv()
    cols_copy = pltpu.make_async_copy(colrecv, cols_s, loc_sem.at[10])
    cols_copy.start()
    table_copy.wait()
    cols_copy.wait()
    cols = [my_col] + [cols_s[NX - j - 1, 0, 0] for j in range(1, NX)]

    def owner_at(d):
        return lax.rem(gy + NY - d, NY) * NX + gx

    def within_of(j, d):
        return tbl_s[0, cols[j], owner_at(d)]

    sent = [[], []]

    def serve(c, *slots_of):
        n, start = len(slots_of), place[slots_of[0]]
        for e in range(1, NX):
            for d in slots_of:
                std[c, e - 1, place[d]] = chunk[c][d][jnp.maximum(within_of(e, d) - 1, 0)]
            x = remote(
                std.at[c, e - 1, pl.ds(start, n)], got[c].at[pl.ds(e * NY + start, n)],
                xd_s.at[c, e - 1, start], xd_r.at[c, e - 1, start], along_x(e),
            )
            x.start()
            sent[c].append(x)
        for d in slots_of:
            got[c][place[d]] = chunk[c][d][jnp.maximum(within_of(0, d) - 1, 0)]

    def step(c, d):
        forward(c, d)
        serve(c, d, NY - d)

    def last(c):
        ag[c][4, 0].wait_recv()
        ag[c][4, 1].wait_recv()
        serve(c, 4)

    def place_of(m):
        owner = home_s[my_col, m] >> 2
        d = (gy - (owner >> 2)) & 7
        at = jnp.where(d == 0, 0, jnp.where(d <= 4, 2 * d - 1, 16 - 2 * d))
        return ((gx - (owner & 3)) & 3) * NY + at

    own_loads[0].wait()
    serve(0, 0)

    def build(i, _):
        start = pl.multiple_of(i * 32, 32)
        row = lax.broadcasted_iota(jnp.int32, (32, 256), 0) + start
        colm = lax.broadcasted_iota(jnp.int32, (32, 256), 1)
        forward = jnp.where(colm < LZ - 1, band(row - colm, FORWARD), 0.0)
        dz[pl.ds(start, 32), :] = forward
        dzb[pl.ds(start, 32), :] = band(row - colm, BACKWARD)
        same = (row >> 5) == (colm >> 5)
        my[pl.ds(start, 32), :] = jnp.where(same, band(colm - row, FORWARD), 0.0)
        return 0

    lax.fori_loop(0, 8, build, 0)

    def build_back(i, _):
        start = pl.multiple_of(i * 32, 32)
        row = lax.broadcasted_iota(jnp.int32, (32, 256), 0) + start
        colm = lax.broadcasted_iota(jnp.int32, (32, 256), 1)
        same = (row >> 4) == (colm >> 5)
        delta = ((colm & 31) - H) - (row & 15)
        myb[pl.ds(start, 32), :] = jnp.where(same, band(delta, BACKWARD), 0.0)
        return 0

    lax.fori_loop(0, 4, build_back, 0)

    step(0, 1)

    loads[0].wait()
    loads[1].wait()

    def forward_z(f):
        def body(g, _):
            block = u[f, pl.ds(H + 8 * g, 8), H : H + LY, :].reshape(8 * LY, LZ)
            fz[f, pl.ds(8 * g, 8)] = dot(block, dz[...]).reshape(8, LY, LZ)
            return 0

        lax.fori_loop(0, 4, body, 0)

    for c in small[3:]:
        c.wait()
    cell_s = src_cell[0]
    amp = src_amp[0]
    shape = (8, LY, LZ)
    iota_x = lax.broadcasted_iota(jnp.int32, shape, 0)
    iota_y = lax.broadcasted_iota(jnp.int32, shape, 1)
    iota_z = lax.broadcasted_iota(jnp.int32, shape, 2)
    flat = ((iota_x + px * LX) * (NPY * LY) + iota_y + py * LY) * LZ + iota_z
    note_x = [
        remote(note, notes.at[0, e], nx_s.at[e - 1], nx_r.at[e - 1], along_x(e)) for e in range(1, NX)
    ]
    note_y = {}
    for d, k, target in ((1, 0, up), (2, 1, up), (3, 2, up), (4, 3, up), (7, 0, down), (6, 7, down), (5, 6, down)):
        note_y[d] = remote(notes.at[k], notes.at[d], ny_s.at[d], ny_r.at[d], target)

    def write_note():
        def body(g, total):
            block = u[1, pl.ds(H + 8 * g, 8), H : H + LY, :]
            hit = jnp.where(flat + g * (8 * NPY * LY * LZ) == cell_s, block, 0.0)
            return total + jnp.sum(hit, axis=0)

        value = jnp.sum(lax.fori_loop(0, 4, body, jnp.zeros((LY, LZ), jnp.float32))) * amp
        x, y, z = (cell_s >> 14) - px * LX, ((cell_s >> 8) & 63) - py * LY, cell_s & 255
        mine = (x >= 0) & (x < LX) & (y >= 0) & (y < LY)
        block = home_s[my_col, z >> 4]
        at = jnp.where(mine, block * (LX * LZ) + x * LZ + y * BZ + (z & 15), -1)
        row = lax.broadcasted_iota(jnp.int32, (8, 128), 0)
        tile = jnp.where(row == 0, at.astype(jnp.float32), value)
        note[...] = tile
        notes[0, 0] = tile
        for c in note_x:
            c.start()

    forward_z(0)
    step(0, 2)
    write_note()
    step(0, 3)
    first(1)
    for c in note_x:
        c.wait_recv()
    note_y[1].start()
    note_y[7].start()
    forward_z(1)

    cell = rec_cell[...]
    cell_x = (cell >> 14) - px * LX
    cell_y = ((cell >> 8) & 63) - py * LY
    cell_z = cell & 255
    here = (cell_x >= 0) & (cell_x < LX) & (cell_y >= 0) & (cell_y < LY)
    spot = jnp.where(here, cell_x * LY + cell_y, -1)
    by_depth = jnp.where(lax.broadcasted_iota(jnp.int32, (LZ, 256), 0) == cell_z, rec_val[...], 0.0)
    loads[2].wait()
    loads[3].wait()

    def bases(g, _):
        start = pl.multiple_of(g * 128, 128)
        at = (lax.broadcasted_iota(jnp.int32, (128, 256), 0) + start == spot).astype(jnp.float32)
        added = lax.dot_general(
            at, by_depth, (((1,), (1,)), ((), ())), precision=HIGHEST, preferred_element_type=jnp.float32
        ).reshape(8, LY, LZ)
        rows = pl.ds(8 * g, 8)
        nx[0, rows] = 2.0 * u[0, pl.ds(H + 8 * g, 8), H : H + LY, :] - nx[0, rows]
        nx[1, rows] = 2.0 * u[1, pl.ds(H + 8 * g, 8), H : H + LY, :] - nx[1, rows] + added
        return 0

    lax.fori_loop(0, 4, bases, 0)

    last(0)
    own_loads[1].wait()
    serve(1, 0)

    def forward_xy(f):
        def body_x(k, _):
            total = None
            for r, weight in enumerate(COEFS, 1):
                term = weight * (u[f, k + 4 + r, H : H + LY, :] - u[f, k + 5 - r, H : H + LY, :])
                total = term if total is None else total + term
            fx[f, k] = total
            return 0

        lax.fori_loop(0, LX + 7, body_x, 0)

        def body_y(g, _):
            block = u[f, pl.ds(H + 8 * g, 8)].reshape(8 * (LY + 2 * H), LZ)
            fy[f, pl.ds(8 * g, 8)] = dot(my[...], block).reshape(8, LY + 2 * H, LZ)
            return 0

        lax.fori_loop(0, 4, body_y, 0)

    wait_sides(halos[0])
    forward_xy(0)
    step(1, 1)

    def to_pencil(c, store):
        for x in sent[c]:
            x.wait_recv()
        places = [place_of(m) for m in range(BLOCKS)]

        def body(k, _):
            tiles = []
            for m in range(BLOCKS):
                slab = got[c][places[m], pl.ds(pl.multiple_of(8 * k, 8), 8), :]
                tiles.append([slab[:, :128], slab[:, 128:]])
            tiles = swap_groups(tiles)
            for y in range(LY):
                for half in range(2):
                    tmp[half, pl.ds(k * 128 + y, 8, stride=16), :] = tiles[y][half]
            for half in range(2):
                rows = tmp[half, pl.ds(pl.multiple_of(k * 128, 128), 128), :]
                store(k, half, rows.reshape(8, LY, 128))
            return 0

        lax.fori_loop(0, 4, body, 0)

    def store_rho(g, half, value):
        rho[pl.ds(H + 8 * g, 8), H : H + LY, half * 128 : half * 128 + 128] = value

    def store_vel(g, half, value):
        vel[pl.ds(8 * g, 8), :, half * 128 : half * 128 + 128] = value

    to_pencil(0, store_rho)

    def pack(i, _):
        sy[0, i, 0:4, :] = rho[H + i, H + 12 : H + 16, :]
        sy[0, i, 4:8, :] = rho[H + 16 + i, H + 12 : H + 16, :]
        sy[1, i, 0:4, :] = rho[H + i, H : H + 4, :]
        sy[1, i, 4:8, :] = rho[H + 16 + i, H : H + 4, :]
        return 0

    lax.fori_loop(0, 16, pack, 0)
    rho_halo = {
        "py_up": remote(sy.at[0], hy.at[0], dh_s.at[0], dh_r.at[0], sides["py_up"][2]),
        "py_down": remote(sy.at[1], hy.at[1], dh_s.at[1], dh_r.at[1], sides["py_down"][2]),
        "px_up": remote(rho.at[pl.ds(H + LX - 4, 4), pl.ds(H, LY), :], rho.at[pl.ds(H - 4, 4), pl.ds(H, LY), :], dh_s.at[2], dh_r.at[2], sides["px_up"][2]),
        "px_down": remote(rho.at[pl.ds(H, 4), pl.ds(H, LY), :], rho.at[pl.ds(H + LX, 4), pl.ds(H, LY), :], dh_s.at[3], dh_r.at[3], sides["px_down"][2]),
    }
    start_sides(rho_halo)
    step(1, 2)
    for d, k in ((1, 2), (7, 6)):
        note_y[d].wait_recv()
        note_y[k].start()

    def depth_part(f, g):
        block = rho[pl.ds(H + 8 * g, 8), H : H + LY, :].reshape(8 * LY, LZ)
        scale = 2.0 / (block + pltpu.roll(block, LZ - 1, 1))
        rows = pl.ds(8 * g, 8)
        flux = fz[f, rows].reshape(8 * LY, LZ) * scale
        lap[f, rows] = dot(flux, dzb[...]).reshape(8, LY, LZ)

    def depth_parts(f):
        def body(g, _):
            depth_part(f, g)
            return 0

        lax.fori_loop(0, 4, body, 0)

    depth_parts(0)
    step(1, 3)
    for d, k in ((2, 3), (6, 5)):
        note_y[d].wait_recv()
        note_y[k].start()

    wait_sides(halos[1])
    forward_xy(1)
    depth_parts(1)
    note_y[3].wait_recv()
    note_y[4].start()
    last(1)

    wait_sides(rho_halo)

    @pl.when(py > 0)
    def _():
        def body(i, _):
            rho[H + i, H - 4 : H, :] = hy[0, i, 0:4, :]
            rho[H + 16 + i, H - 4 : H, :] = hy[0, i, 4:8, :]
            return 0

        lax.fori_loop(0, 16, body, 0)

    @pl.when(py < NPY - 1)
    def _():
        def body(i, _):
            rho[H + i, H + LY : H + LY + 4, :] = hy[1, i, 0:4, :]
            rho[H + 16 + i, H + LY : H + LY + 4, :] = hy[1, i, 4:8, :]
            return 0

        lax.fori_loop(0, 16, body, 0)

    def flux_x(f):
        def body(k, _):
            face = px * LX + k - 4
            open_x = (face >= 0) & (face <= NPX * LX - 2)
            scale = jnp.where(open_x, 2.0 / (rho[k + 4, H : H + LY, :] + rho[k + 5, H : H + LY, :]), 0.0)
            fx[f, k] = fx[f, k] * scale
            return 0

        lax.fori_loop(0, LX + 7, body, 0)

    rows_y = lax.broadcasted_iota(jnp.int32, (LY + 2 * H, LZ), 0) - H
    face_y = rows_y + py * LY
    open_y = (rows_y >= -4) & (rows_y < LY + 3) & (face_y >= 0) & (face_y <= NPY * LY - 2)

    def flux_y(f):
        def body(i, _):
            line = rho[H + i]
            scale = jnp.where(open_y, 2.0 / (line + pltpu.roll(line, LY + 2 * H - 1, 0)), 0.0)
            fy[f, i] = fy[f, i] * scale
            return 0

        lax.fori_loop(0, LX, body, 0)

    flux_x(0)
    flux_y(0)

    def laplacian(f, g):
        block = fy[f, pl.ds(8 * g, 8)].reshape(8 * (LY + 2 * H), LZ)
        total = lap[f, pl.ds(8 * g, 8)] + dot(myb[...], block).reshape(8, LY, LZ)
        for r, weight in enumerate(COEFS, 1):
            total = total + weight * (fx[f, pl.ds(8 * g + 3 + r, 8)] - fx[f, pl.ds(8 * g + 4 - r, 8)])
        return total

    def source_field(g, _):
        rows = pl.ds(8 * g, 8)
        change = laplacian(0, g)
        lap[0, rows] = change
        value = change * u[1, pl.ds(H + 8 * g, 8), H : H + LY, :]
        for half in range(2):
            tmp[half, pl.ds(pl.multiple_of(g * 128, 128), 128), :] = value[:, :, half * 128 : half * 128 + 128].reshape(128, 128)
        tiles = []
        for y in range(LY):
            tiles.append([tmp[half, pl.ds(g * 128 + y, 8, stride=16), :] for half in range(2)])
        tiles = swap_groups(tiles)
        for m in range(BLOCKS):
            for half in range(2):
                con[m, pl.ds(pl.multiple_of(8 * g, 8), 8), half * 128 : half * 128 + 128] = tiles[m][half]
        return 0

    xg = {}

    lax.fori_loop(0, 4, source_field, 0)

    def send_back(*slots_of):
        n, start = len(slots_of), place[slots_of[0]]
        for e in range(1, NX):
            for d in slots_of:
                owner = lax.rem(gy + NY - d, NY) * NX + lax.rem(gx + e, NX)
                gst[e - 1, place[d]] = con[tbl_s[1, my_col, owner]]
            c = remote(
                gst.at[e - 1, pl.ds(start, n)], grecv.at[e - 1, pl.ds(start, n)],
                xg_s.at[e - 1, start], xg_r.at[e - 1, start], along_x(e),
            )
            c.start()
            xg[e, slots_of[0]] = c

    for group in ((4,), (3, 5), (2, 6), (1, 7), (0,)):
        send_back(*group)

    def scaled(g):
        v = vel[pl.ds(8 * g, 8)]
        return COURANT2 * (rho[pl.ds(H + 8 * g, 8), H : H + LY, :] * v * v)

    def update_source(g, _):
        rows = pl.ds(8 * g, 8)
        change = scaled(g) * lap[0, rows] - jnp.where(flat + g * (8 * NPY * LY * LZ) == cell_s, amp, 0.0)
        nx[0, rows] = nx[0, rows] + change
        return 0

    def update_adjoint(g, _):
        rows = pl.ds(8 * g, 8)
        nx[1, rows] = nx[1, rows] + scaled(g) * laplacian(1, g)
        return 0

    def sources_of(w):
        row = lax.broadcasted_iota(jnp.int32, (LX, 128), 0)
        lane = lax.broadcasted_iota(jnp.int32, (LX, 128), 1)
        cells = ((shot * HELD + w) * LX + row) * LZ + lane

        def body(r, totals):
            at = notes[r // NX, lax.rem(r, NX), 0:1, :].astype(jnp.int32)
            value = notes[r // NX, lax.rem(r, NX), 1:2, :]
            return tuple(
                total + jnp.where(cells + half * 128 == at, value, 0.0) for half, total in enumerate(totals)
            )

        zero = jnp.zeros((LX, 128), jnp.float32)
        totals = lax.fori_loop(0, NX * NY, body, (zero, zero))
        for half in range(2):
            spike[w, :, half * 128 : half * 128 + 128] = totals[half]

    def collect(*slots_of):
        for e in range(1, NX):
            xg[e, slots_of[0]].wait_recv()
        for d in slots_of:
            values = [con[tbl_s[1, my_col, owner_at(d)]]] + [grecv[NX - j - 1, place[d]] for j in range(1, NX)]
            picks = [within_of(j, d) for j in range(NX)]
            for w in range(HELD):
                total = None
                for j in range(NX):
                    term = jnp.where(picks[j] == w + 1, values[j], 0.0)
                    total = term if total is None else total + term
                part[d][w] = total

    ring = {}
    for d, to, target in ((4, 3, down), (3, 2, down), (2, 1, down), (1, 0, down), (4, 5, up), (5, 6, up), (6, 7, up), (7, 8, up)):
        for w in range(2):
            if d == 4 and w != (0 if to == 3 else 1):
                continue
            ring[to, w] = remote(
                part[d].at[halves[w]], rs.at[to, halves[w]], rs_s.at[to, w], rs_r.at[to, w], target
            )

    def add(d, w):
        ring[d, w].wait_recv()
        rows = slice(2 * w, 2 * w + 2)
        part[d][rows] = part[d][rows] + rs[d, rows]

    for d in (4, 5):
        note_y[d].wait_recv()
    for w in range(2):
        sources_of(w)
    flux_x(1)
    flux_y(1)
    collect(4)
    ring[3, 0].start()
    ring[5, 1].start()
    collect(3, 5)
    ring[2, 1].start()
    ring[6, 0].start()
    for w in range(2, HELD):
        sources_of(w)
    add(3, 0)
    ring[2, 0].start()
    add(5, 1)
    ring[6, 1].start()
    collect(2, 6)
    add(2, 1)
    ring[1, 1].start()
    add(6, 0)
    ring[7, 0].start()
    add(2, 0)
    ring[1, 0].start()
    add(6, 1)
    ring[7, 1].start()
    to_pencil(1, store_vel)
    collect(1, 7)
    add(1, 1)
    ring[0, 1].start()
    add(7, 0)
    ring[8, 0].start()
    add(1, 0)
    ring[0, 0].start()
    add(7, 1)
    ring[8, 1].start()
    collect(0)
    loads[4].wait()

    def settle(w, _):
        own_vel = chunk[1][0][w]
        gin[w] = gin[w] - (2.0 / own_vel) * spike[w]
        spike[w] = (2.0 * COURANT2) * (chunk[0][0][w] * own_vel)
        return 0

    lax.fori_loop(0, HELD, settle, 0)
    lax.fori_loop(0, 4, update_source, 0)
    out_f = pltpu.make_async_copy(nx.at[0], fwd_out, out_sem.at[0])
    out_f.start()
    lax.fori_loop(0, 4, update_adjoint, 0)
    out_a = pltpu.make_async_copy(nx.at[1], adj_out, out_sem.at[1])
    out_a.start()
    for w in (1, 0):
        ring[0, w].wait_recv()
        ring[8, 1 - w].wait_recv()
    for w in range(HELD):
        gin[w] = gin[w] + spike[w] * (part[0][w] + (rs[0, w] + rs[8, w]))
    out_g = pltpu.make_async_copy(gin, grad_out, out_sem.at[2])
    out_g.start()

    for c in col_copies + note_x + list(note_y.values()) + sent[0] + sent[1] + list(xg.values()) + list(ring.values()):
        c.wait_send()
    for copies in ag:
        for c in copies.values():
            c.wait_send()
    finish_sides(halos[0])
    finish_sides(halos[1])
    finish_sides(rho_halo)
    out_f.wait()
    out_a.wait()
    out_g.wait()


def shards(
    fwd_now,
    fwd_next,
    adj_now,
    adj_next,
    velocity,
    density,
    gradient_in,
    block_home,
    aperture_col,
    source_cell,
    source_amp,
    receiver_cell,
    receiver_residual,
):
    f32, i32 = jnp.float32, jnp.int32
    any_space = pl.BlockSpec(memory_space=pl.ANY)
    pencil = (LX, LY, LZ)
    blocks = (HELD, LX, LZ)
    V = pltpu.VMEM
    D = pltpu.SemaphoreType.DMA
    scratch = [
        V((2, LX + 2 * H, LY + 2 * H, LZ), f32),
        V((2,) + pencil, f32),
        V((2, LX + 8, LY, LZ), f32),
        V((2, LX, LY + 2 * H, LZ), f32),
        V((2,) + pencil, f32),
        V((2,) + pencil, f32),
        V((LX + 2 * H, LY + 2 * H, LZ), f32),
        V(pencil, f32),
    ]
    scratch += [
        V((2, NX - 1, NY, LX, LZ), f32),
        V((NX * NY, LX, LZ), f32),
        V((NX * NY, LX, LZ), f32),
        V((2, LX * LY, 128), f32),
        V((2, 16, 8, LZ), f32),
        V((2, 16, 8, LZ), f32),
        V((BLOCKS, LX, LZ), f32),
        V((NX - 1, NY, LX, LZ), f32),
        V((NX - 1, NY, LX, LZ), f32),
        V(blocks, f32),
        V((9,) + blocks, f32),
        V((256, 256), f32),
        V((256, 256), f32),
        V((256, 256), f32),
        V((128, 256), f32),
        V((2, 8, 128), i32),
        pltpu.SMEM((2, 8, 128), i32),
        V((8, 128), i32),
        V((NX - 1, 8, 128), i32),
        pltpu.SMEM((NX - 1, 8, 128), i32),
        D((11,)),
        D((2, 8, 2)), D((2, 8, 2)),
        D((2, 3, 8)), D((2, 3, 8)),
        D((3, 8)), D((3, 8)),
        D((9, 2)), D((9, 2)),
        D((2, 4)), D((2, 4)),
        D((4,)), D((4,)),
        D((3,)), D((3,)),
        D((3,)),
        V((8, 16), i32),
        pltpu.SMEM((8, 16), i32),
        pltpu.SMEM((1,), i32),
        pltpu.SMEM((1,), i32),
        pltpu.SMEM((1,), f32),
        V((1, 256), i32),
        V((1, 256), f32),
        D((7,)),
        V((8, 128), f32),
        V((NY, NX, 8, 128), f32),
        V(blocks, f32),
        D((3,)), D((3,)),
        D((8,)), D((8,)),
    ]
    scratch += [V(blocks, f32) for _ in range(24)]
    fwd, adj, grad = pl.pallas_call(
        kernel,
        out_shape=(
            jax.ShapeDtypeStruct(pencil, f32),
            jax.ShapeDtypeStruct(pencil, f32),
            jax.ShapeDtypeStruct(blocks, f32),
        ),
        in_specs=[any_space] * 13,
        out_specs=(any_space, any_space, any_space),
        scratch_shapes=scratch,
        compiler_params=pltpu.CompilerParams(
            collective_id=0, has_side_effects=True, vmem_limit_bytes=62 * 2**20
        ),
        name="wave_step",
    )(
        fwd_now[0], adj_now[0], fwd_next[0], adj_next[0], velocity, density, gradient_in,
        block_home, aperture_col, source_cell, source_amp, receiver_cell, receiver_residual,
    )
    return fwd[None], adj[None], grad


def solution(mesh):
    in_specs = (
        P("shot", "px", "py", None),
        P("shot", "px", "py", None),
        P("shot", "px", "py", None),
        P("shot", "px", "py", None),
        P("shot", "px", "py"),
        P("shot", "px", "py"),
        P("shot", "px", "py"),
        P(),
        P("shot"),
        P("shot"),
        P("shot"),
        P("shot", None),
        P("shot", None),
    )
    out_specs = (P("shot", "px", "py", None), P("shot", "px", "py", None), P("shot", "px", "py"))
    return jax.shard_map(shards, mesh=mesh, in_specs=in_specs, out_specs=out_specs, check_vma=False)
```

time: 91 us -> 79.3 us (0.87)
  local copies, waits for them, and re-layouts: 9.81 us -> 3.61 us
  Pallas kernels: 78.2 us -> 72.9 us
    unnamed x23 -> x7, local copies, waits for them, and re-layouts: 9.81 us -> 3.61 us
    pallas_call x1, Pallas kernels: 78.2 us -> 72.9 us  [shards(): pl.pallas_call(kernel, out_shape=(jax.ShapeDtypeStruct(pencil, f32), jax....]
where the time goes in v2:
time: 79.3 us; the launch traced here: 79.1 us
  Pallas kernels  72.9 us (92%)
  local copies, waits for them, and re-layouts  3.61 us (5%)
  between operations  2.59 us (3%)
    pallas_call x1, Pallas kernels, shards(): pl.pallas_call(kernel, out_shape=(jax.ShapeDtypeStruct(pencil, f32), jax....  72.9 us
    unnamed x7, local copies, waits for them, and re-layouts  3.61 us

profile of v2, /device:TPU:128, one launch (start us, length us, event | category | flops | bytes accessed | tf_op | source)
XLA Modules:
  0.0 79.1 jit_solution(1755183538193314579)
XLA Ops:
  2.6 72.9 %wave_step.1 = (f32[32,16,256]{2,1,0:T(8,128)}, f32[32,16,256]{2,1,0:T(8,128)}, f32[4,32,256]{2,1,0:T(8,128)}) custom-call(f32[32,16,256]{2,1,0:T(8,128)} %bitcast.8, f32[32,16,256]{2,1,0:T(8,128)} %bitcast.9, f32[32,16,256]{2,1,0:T(8,128)} %bitcast.10, f32[32,16,256]{2,1,0:T(8,128)} %bitcast.11, f32[4,32,256]{2,1,0:T(8,128)} %velocity.1, ...), custom_call_target="tpu_custom_call" | custom-call | tf_op jit(solution)/shard_map/wave_step/pallas_call | solution.py:783
  75.5 0.0 copy-start
  75.5 1.9 %copy.22 = f32[1,32,16,256]{3,2,1,0:T(8,128)} copy(f32[1,32,16,256]{3,2,1,0:T(8,128)} %bitcast.7) | data formatting | bytes 1048576
  77.4 0.0 copy-done
  77.4 0.0 copy-start.1
  77.4 0.8 %copy.23 = f32[1,32,16,256]{3,2,1,0:T(8,128)} copy(f32[1,32,16,256]{3,2,1,0:T(8,128)S(1)} %bitcast.6) | data formatting | bytes 1048576
  78.2 0.2 copy-done.1
  78.5 0.7 copy.24
Async XLA Ops:
  75.5 1.9 %copy-start = (f32[32,16,256]{2,1,0:T(8,128)S(1)}, f32[32,16,256]{2,1,0:T(8,128)}, u32[]{:S(2)}) copy-start(f32[32,16,256]{2,1,0:T(8,128)} %get-tuple-element.7) | copy-start | bytes 1572868
  77.4 1.0 %copy-start.1 = (f32[4,32,256]{2,1,0:T(8,128)S(1)}, f32[4,32,256]{2,1,0:T(8,128)}, u32[]{:S(2)}) copy-start(f32[4,32,256]{2,1,0:T(8,128)} %get-tuple-element.14) | copy-start | bytes 393220

commit v3 on v2

--- a/solution.py
+++ b/solution.py
@@ -207,7 +207,6 @@
 
     halos = [halo(0, fwd_now), halo(1, adj_now)]
     start_sides(halos[0])
-    start_sides(halos[1])
     small[1].wait()
     small[2].wait()
     lane8 = lax.broadcasted_iota(jnp.int32, (8, 128), 1)
@@ -475,14 +474,12 @@
         note_y[d].wait_recv()
         note_y[k].start()
 
-    wait_sides(halos[1])
-    forward_xy(1)
-    depth_parts(1)
     note_y[3].wait_recv()
     note_y[4].start()
     last(1)
 
     wait_sides(rho_halo)
+    start_sides(halos[1])
 
     @pl.when(py > 0)
     def _():
@@ -634,8 +631,7 @@
         note_y[d].wait_recv()
     for w in range(2):
         sources_of(w)
-    flux_x(1)
-    flux_y(1)
+    depth_parts(1)
     collect(4)
     ring[3, 0].start()
     ring[5, 1].start()
@@ -680,6 +676,10 @@
     lax.fori_loop(0, 4, update_source, 0)
     out_f = pltpu.make_async_copy(nx.at[0], fwd_out, out_sem.at[0])
     out_f.start()
+    wait_sides(halos[1])
+    forward_xy(1)
+    flux_x(1)
+    flux_y(1)
     lax.fori_loop(0, 4, update_adjoint, 0)
     out_a = pltpu.make_async_copy(nx.at[1], adj_out, out_sem.at[1])
     out_a.start()
@@ -798,6 +798,38 @@
         fwd_now[0], adj_now[0], fwd_next[0], adj_next[0], velocity, density, gradient_in,
         block_home, aperture_col, source_cell, source_amp, receiver_cell, receiver_residual,
     )
+    def settle_results(*refs):
+        held, ins, outs = refs[6:9], refs[9], refs[10]
+        coming, going = [], []
+        for i in range(3):
+            src, buf, dst = refs[i], held[i], refs[3 + i]
+            pieces = 4 if i < 2 else 2
+            rows = buf.shape[0] // pieces
+            for k in range(pieces):
+                at, n = pl.ds(k * rows, rows), len(coming)
+                coming.append(pltpu.make_async_copy(src.at[at], buf.at[at], ins.at[n]))
+                going.append(pltpu.make_async_copy(buf.at[at], dst.at[at], outs.at[n]))
+        for c in coming:
+            c.start()
+        for c, g in zip(coming, going):
+            c.wait()
+            g.start()
+        for g in going:
+            g.wait()
+
+    fwd, adj, grad = pl.pallas_call(
+        settle_results,
+        out_shape=(
+            jax.ShapeDtypeStruct(pencil, f32),
+            jax.ShapeDtypeStruct(pencil, f32),
+            jax.ShapeDtypeStruct(blocks, f32),
+        ),
+        in_specs=[any_space] * 3,
+        out_specs=(any_space, any_space, any_space),
+        scratch_shapes=[V(pencil, f32), V(pencil, f32), V(blocks, f32), D((10,)), D((10,))],
+        compiler_params=pltpu.CompilerParams(vmem_limit_bytes=62 * 2**20),
+        name="results",
+    )(fwd, adj, grad)
     return fwd[None], adj[None], grad
 
 

time: 79.3 us -> 76.1 us (0.960)
  local copies, waits for them, and re-layouts: 3.61 us -> 0 us
    unnamed x7 -> x0, local copies, waits for them, and re-layouts: 3.61 us -> none
    pallas_call x0 -> x1, Pallas kernels: none -> 2.16 us  [shards(): pl.pallas_call(settle_results, out_shape=(jax.ShapeDtypeStruct(pencil, f3...]
    pallas_call x1, Pallas kernels: 72.9 us -> 71.2 us  [shards(): pl.pallas_call(kernel, out_shape=(jax.ShapeDtypeStruct(pencil, f32), jax....]
where the time goes in v3:
time: 76.1 us; the launch traced here: 75.9 us
  Pallas kernels  73.3 us (96%)
  between operations  2.58 us (3%)
    pallas_call x1, Pallas kernels, shards(): pl.pallas_call(kernel, out_shape=(jax.ShapeDtypeStruct(pencil, f32), jax....  71.2 us
    pallas_call x1, Pallas kernels, shards(): pl.pallas_call(settle_results, out_shape=(jax.ShapeDtypeStruct(pencil, f3...  2.16 us

profile of v3, /device:TPU:128, one launch (start us, length us, event | category | flops | bytes accessed | tf_op | source)
XLA Modules:
  0.0 75.9 jit_solution(899193408223587046)
XLA Ops:
  2.6 71.2 %wave_step.1 = (f32[32,16,256]{2,1,0:T(8,128)}, f32[32,16,256]{2,1,0:T(8,128)}, f32[4,32,256]{2,1,0:T(8,128)}) custom-call(f32[32,16,256]{2,1,0:T(8,128)} %bitcast.6, f32[32,16,256]{2,1,0:T(8,128)} %bitcast.7, f32[32,16,256]{2,1,0:T(8,128)} %bitcast.8, f32[32,16,256]{2,1,0:T(8,128)} %bitcast.9, f32[4,32,256]{2,1,0:T(8,128)} %velocity.1, ...), custom_call_target="tpu_custom_call" | custom-call | tf_op jit(solution)/shard_map/wave_step/pallas_call | solution.py:783
  73.8 2.2 %results.1 = (f32[32,16,256]{2,1,0:T(8,128)}, f32[32,16,256]{2,1,0:T(8,128)}, f32[4,32,256]{2,1,0:T(8,128)}) custom-call(f32[32,16,256]{2,1,0:T(8,128)} %get-tuple-element.9.refs_0_, f32[32,16,256]{2,1,0:T(8,128)} %get-tuple-element.10.refs_1_, f32[4,32,256]{2,1,0:T(8,128)} %get-tuple-element.11.refs_2_), custom_call_target="tpu_custom_call" | custom-call | tf_op jit(solution)/shard_map/results/pallas_call | solution.py:820

commit v4 on v3

--- a/solution.py
+++ b/solution.py
@@ -347,9 +347,9 @@
 
     forward_z(0)
     step(0, 2)
+    first(1)
     write_note()
     step(0, 3)
-    first(1)
     for c in note_x:
         c.wait_recv()
     note_y[1].start()

time: 76.1 us -> 76.5 us (level)
  no operation moved by 1% of the time
where the time goes in v4:
time: 76.5 us; the launch traced here: 76.3 us
  Pallas kernels  73.7 us (96%)
  between operations  2.58 us (3%)
    pallas_call x1, Pallas kernels, shards(): pl.pallas_call(kernel, out_shape=(jax.ShapeDtypeStruct(pencil, f32), jax....  71.6 us
    pallas_call x1, Pallas kernels, shards(): pl.pallas_call(settle_results, out_shape=(jax.ShapeDtypeStruct(pencil, f3...  2.16 us

profile of v4, /device:TPU:128, one launch (start us, length us, event | category | flops | bytes accessed | tf_op | source)
XLA Modules:
  0.0 76.3 jit_solution(12395766585480510374)
XLA Ops:
  2.6 71.6 %wave_step.1 = (f32[32,16,256]{2,1,0:T(8,128)}, f32[32,16,256]{2,1,0:T(8,128)}, f32[4,32,256]{2,1,0:T(8,128)}) custom-call(f32[32,16,256]{2,1,0:T(8,128)} %bitcast.6, f32[32,16,256]{2,1,0:T(8,128)} %bitcast.7, f32[32,16,256]{2,1,0:T(8,128)} %bitcast.8, f32[32,16,256]{2,1,0:T(8,128)} %bitcast.9, f32[4,32,256]{2,1,0:T(8,128)} %velocity.1, ...), custom_call_target="tpu_custom_call" | custom-call | tf_op jit(solution)/shard_map/wave_step/pallas_call | solution.py:783
  74.1 2.2 %results.1 = (f32[32,16,256]{2,1,0:T(8,128)}, f32[32,16,256]{2,1,0:T(8,128)}, f32[4,32,256]{2,1,0:T(8,128)}) custom-call(f32[32,16,256]{2,1,0:T(8,128)} %get-tuple-element.9.refs_0_, f32[32,16,256]{2,1,0:T(8,128)} %get-tuple-element.10.refs_1_, f32[4,32,256]{2,1,0:T(8,128)} %get-tuple-element.11.refs_2_), custom_call_target="tpu_custom_call" | custom-call | tf_op jit(solution)/shard_map/results/pallas_call | solution.py:820
